TPU v7x, 32 devices: a whole 2x2x4 slice. The times are simulated.
32 devices in a mesh: replica: 8 (over y, x, core), group: 4 (over z).
Axes of the slice: x: 2, y: 2, z: 4, core: 2. Of those that a mesh axis runs over, the one named last changes fastest.
Arguments:
- tokens: bfloat16 [8192, 2048], P(('replica', 'group')), may hold values from -6 to 6
- cotangent: bfloat16 [8192, 2048], P(('replica', 'group')), may hold values from -6 to 6
- lengths: int32 [8, 3], P('replica'), may hold values from 1 to 512, 1024 in all within a row
- packing: int32 [8, 1024], P('replica'), may hold values from 0 to 1023, each once within a row
- attn_gain: float32 [2048], P('group'), may hold values from 0.1 to 1.9
- w_query: bfloat16 [2048, 2048], P('group'), may hold values from -0.125 to 0.125
- w_key_value: bfloat16 [2048, 2, 512], P('group'), may hold values from -0.125 to 0.125
- w_out: bfloat16 [2048, 2048], P('group'), may hold values from -0.75 to 0.75
- mlp_gain: float32 [2048], P('group'), may hold values from 0.1 to 1.9
- w_gate_up: bfloat16 [2048, 2, 8192], P('group'), may hold values from -0.125 to 0.125
- w_down: bfloat16 [8192, 2048], P('group'), may hold values from -0.0625 to 0.0625
Outputs:
- mixed: bfloat16 [8192, 2048], P(('replica', 'group'))
- layer_input_gradient: bfloat16 [8192, 2048], P(('replica', 'group'))
- attn_gain_grad: float32 [2048], P('group')
- w_query_grad: float32 [2048, 2048], P('group')
- w_key_value_grad: float32 [2048, 2, 512], P('group')
- w_out_grad: float32 [2048, 2048], P('group')
- mlp_gain_grad: float32 [2048], P('group')
- w_gate_up_grad: float32 [2048, 2, 8192], P('group')
- w_down_grad: float32 [8192, 2048], P('group')
Inputs may be any that keep to these rules, and one draw needn't show every extreme that they name: `lengths`: each row sums to 1024 and its largest entry is exactly 512. `packing`: each row holds every number of 0 to 1023 once.
All inputs are finite; a program needn't handle non-finite values.
Results may differ from a plain program's by a relative error of at most 0.035.
Values may be sent and summed in bfloat16 or wider, within the bound.
No kernel may reach another device: no remote copies, remote signals or barrier semaphores. Data moves between devices by JAX's collectives and lax.ppermute only.
A program may use at most 640 MiB of HBM per device.

v0:
```python
import math

import jax
import jax.numpy as jnp
from jax import lax
from jax.sharding import PartitionSpec as P

HEADS = 32
KV_HEADS = 8
HEAD_DIM = 64


EPS = 1e-05
NEG = -1e30


def frequencies(head_size):
    half = head_size // 2
    expo = jnp.arange(half).astype(jnp.float32) * (2.0 / head_size)
    base = jnp.power(jnp.float32(500000.0), -expo)
    wavelen = 2.0 * math.pi / base
    smooth = (8192.0 / wavelen - 1.0) / 3.0
    middle = (1.0 - smooth) * base / 32.0 + smooth * base
    return jnp.where(wavelen < 2048.0, base, jnp.where(wavelen > 8192.0, base / 32.0, middle))


def stream_meta(lengths_row, stream):
    ends = jnp.cumsum(lengths_row)
    past = ends[None, :] <= stream[:, None]
    segment = jnp.sum(past.astype(jnp.int32), axis=1)
    before = jnp.sum(jnp.where(past, lengths_row[None, :], 0), axis=1)
    return (segment, stream - before)


def rope(value, cosine, sine):
    half = value.shape[-1] // 2
    first, second = (value[..., :half], value[..., half:])
    return jnp.concatenate(
        [first * cosine - second * sine, second * cosine + first * sine], axis=-1
    )


def rope_back(grad, cosine, sine):
    half = grad.shape[-1] // 2
    first, second = (grad[..., :half], grad[..., half:])
    return jnp.concatenate(
        [first * cosine + second * sine, second * cosine - first * sine], axis=-1
    )


def rms_normalize_rows(value):
    inverse_rms_value = lax.rsqrt(jnp.mean(value * value, axis=-1, keepdims=True) + EPS)
    return (value * inverse_rms_value, inverse_rms_value)


def rms_norm_backward(normalized_gradient, unit_rms_rows, inverse_rms_value, gain_vector):
    gain_scaled_rows = normalized_gradient * gain_vector
    return inverse_rms_value * (
        gain_scaled_rows
        - unit_rms_rows * jnp.mean(gain_scaled_rows * unit_rms_rows, axis=-1, keepdims=True)
    )


def contract_rows(left, right):
    return lax.dot_general(
        left, right, (((0,), (0,)), ((), ())), preferred_element_type=jnp.float32
    )


def contract_cols(left, right):
    return lax.dot_general(
        left, right, (((1,), (1,)), ((), ())), preferred_element_type=jnp.float32
    )


def local(
    tokens,
    cotangent,
    lengths,
    packing,
    attn_gain,
    w_query,
    w_key_value,
    w_out,
    mlp_gain,
    w_gate_up,
    w_down,
):
    f32 = jnp.float32
    brain_float_sixteen = jnp.bfloat16
    ntok = tokens.shape[0]
    group_tok = packing.shape[1]
    share = HEADS // KV_HEADS
    kv_width = KV_HEADS * HEAD_DIM
    q_width = HEADS * HEAD_DIM
    scale = HEAD_DIM ** (-0.5)
    block = min(512, group_tok)
    nblock = group_tok // block
    seg_all, pos_all = stream_meta(lengths[0], packing[0])
    first_row = lax.axis_index("group") * ntok
    seg_own = lax.dynamic_slice_in_dim(seg_all, first_row, ntok)
    pos_own = lax.dynamic_slice_in_dim(pos_all, first_row, ntok)
    angles = pos_own.astype(f32)[:, None] * frequencies(HEAD_DIM)[None, :]
    cosine = jnp.cos(angles)[:, None, :]
    sine = jnp.sin(angles)[:, None, :]
    seg_blocks = seg_all.reshape(nblock, block)
    pos_blocks = pos_all.reshape(nblock, block)
    hidden_input_rows = tokens.astype(f32)
    first_unit_rms_rows, first_inverse_rms = rms_normalize_rows(hidden_input_rows)
    wq_all, wkv_all, wo_all, first_gain_vector = (
        lax.all_gather(w_query, "group", axis=0, tiled=True),
        lax.all_gather(w_key_value, "group", axis=0, tiled=True),
        lax.all_gather(w_out, "group", axis=0, tiled=True),
        lax.all_gather(attn_gain.astype(jnp.bfloat16), "group", axis=0, tiled=True).astype(
            attn_gain.dtype
        ),
    )
    first_normalized_rows = (first_unit_rms_rows * first_gain_vector).astype(brain_float_sixteen)
    query = jnp.dot(first_normalized_rows, wq_all, preferred_element_type=f32)
    keyval = jnp.einsum("tc,cjk->tjk", first_normalized_rows, wkv_all, preferred_element_type=f32)
    q_rot = rope(query.reshape(ntok, HEADS, HEAD_DIM), cosine, sine).astype(brain_float_sixteen)
    q_rot = q_rot.reshape(ntok, KV_HEADS, share, HEAD_DIM)
    k_rot = rope(keyval[:, 0].reshape(ntok, KV_HEADS, HEAD_DIM), cosine, sine).astype(
        brain_float_sixteen
    )
    v_own = keyval[:, 1].astype(brain_float_sixteen)
    keys_all, values_all = (
        lax.all_gather(k_rot.reshape(ntok, kv_width), "group", axis=0, tiled=True),
        lax.all_gather(v_own, "group", axis=0, tiled=True),
    )
    keys_all = keys_all.reshape(nblock, block, KV_HEADS, HEAD_DIM)
    values_all = values_all.reshape(nblock, block, KV_HEADS, HEAD_DIM)

    def scores_of(key_block, seg_keys, pos_keys):
        raw = jnp.einsum("tkgd,skd->kgts", q_rot, key_block, preferred_element_type=f32) * scale
        mask = (seg_own[:, None] == seg_keys[None, :]) & (pos_keys[None, :] <= pos_own[:, None])
        return (jnp.where(mask, raw, NEG), mask)

    def running(carry, item):
        top, total = carry
        key_block, seg_keys, pos_keys = item
        masked, mask = scores_of(key_block, seg_keys, pos_keys)
        new_top = jnp.maximum(top, jnp.max(masked, axis=-1))
        fresh = jnp.sum(jnp.where(mask, jnp.exp(masked - new_top[..., None]), 0.0), axis=-1)
        return ((new_top, total * jnp.exp(top - new_top) + fresh), None)

    stats_shape = (KV_HEADS, share, ntok)
    (top, total), _ = lax.scan(
        running,
        (jnp.full(stats_shape, NEG, f32), jnp.zeros(stats_shape, f32)),
        (keys_all, seg_blocks, pos_blocks),
    )
    lse = top + jnp.log(total)

    def weigh(acc, item):
        key_block, value_block, seg_keys, pos_keys = item
        masked, mask = scores_of(key_block, seg_keys, pos_keys)
        probs = jnp.where(mask, jnp.exp(masked - lse[..., None]), 0.0).astype(brain_float_sixteen)
        return (
            acc + jnp.einsum("kgts,skd->tkgd", probs, value_block, preferred_element_type=f32),
            None,
        )

    attended, _ = lax.scan(
        weigh,
        jnp.zeros((ntok, KV_HEADS, share, HEAD_DIM), f32),
        (keys_all, values_all, seg_blocks, pos_blocks),
    )
    attended_low = attended.reshape(ntok, q_width).astype(brain_float_sixteen)
    residual_after_attention = hidden_input_rows + jnp.dot(
        attended_low, wo_all, preferred_element_type=f32
    )
    wgu_all, wd_all, second_gain_vector = (
        lax.all_gather(w_gate_up, "group", axis=0, tiled=True),
        lax.all_gather(w_down, "group", axis=0, tiled=True),
        lax.all_gather(mlp_gain.astype(jnp.bfloat16), "group", axis=0, tiled=True).astype(
            mlp_gain.dtype
        ),
    )
    second_unit_rms_rows, second_inverse_rms = rms_normalize_rows(residual_after_attention)
    second_normalized_rows = (second_unit_rms_rows * second_gain_vector).astype(brain_float_sixteen)
    gateup = jnp.einsum("tc,cjf->tjf", second_normalized_rows, wgu_all, preferred_element_type=f32)
    gate = gateup[:, 0]
    up_part = gateup[:, 1]
    sigma = jax.nn.sigmoid(gate)
    silu_gate = gate * sigma
    hidden = (silu_gate * up_part).astype(brain_float_sixteen)
    mixed = (residual_after_attention + jnp.dot(hidden, wd_all, preferred_element_type=f32)).astype(
        brain_float_sixteen
    )
    wgu_back, wd_back, second_gain_gradient = (
        lax.all_gather(w_gate_up, "group", axis=0, tiled=True),
        lax.all_gather(w_down, "group", axis=0, tiled=True),
        lax.all_gather(mlp_gain.astype(jnp.bfloat16), "group", axis=0, tiled=True).astype(
            mlp_gain.dtype
        ),
    )
    grad_hidden = contract_cols(cotangent, wd_back)
    grad_gate = grad_hidden * up_part * sigma * (1.0 + gate * (1.0 - sigma))
    grad_up = grad_hidden * silu_gate
    grad_gateup = jnp.stack([grad_gate, grad_up], axis=1).astype(brain_float_sixteen)
    second_normalized_gradient = jnp.einsum(
        "tjf,cjf->tc", grad_gateup, wgu_back, preferred_element_type=f32
    )
    feedforward_gain_slice = jnp.sum(second_normalized_gradient * second_unit_rms_rows, axis=0)
    residual_one_gradient = cotangent.astype(f32) + rms_norm_backward(
        second_normalized_gradient, second_unit_rms_rows, second_inverse_rms, second_gain_gradient
    )
    w_down_grad = lax.psum_scatter(
        contract_rows(hidden, cotangent).astype(jnp.bfloat16),
        "group",
        scatter_dimension=0,
        tiled=True,
    ).astype(jnp.float32)
    w_gate_up_grad = lax.psum_scatter(
        jnp.einsum(
            "tc,tjf->cjf", second_normalized_rows, grad_gateup, preferred_element_type=f32
        ).astype(jnp.bfloat16),
        "group",
        scatter_dimension=0,
        tiled=True,
    ).astype(jnp.float32)
    wq_back, wkv_back, wo_back, first_gain_gradient = (
        lax.all_gather(w_query, "group", axis=0, tiled=True),
        lax.all_gather(w_key_value, "group", axis=0, tiled=True),
        lax.all_gather(w_out, "group", axis=0, tiled=True),
        lax.all_gather(attn_gain.astype(jnp.bfloat16), "group", axis=0, tiled=True).astype(
            attn_gain.dtype
        ),
    )
    grad_attn = residual_one_gradient.astype(brain_float_sixteen)
    grad_heads = (
        contract_cols(grad_attn, wo_back)
        .astype(brain_float_sixteen)
        .reshape(ntok, KV_HEADS, share, HEAD_DIM)
    )
    delta = jnp.einsum("tkgd,tkgd->kgt", grad_heads.astype(f32), attended)

    def backward_block(grad_q, item):
        key_block, value_block, seg_keys, pos_keys = item
        masked, mask = scores_of(key_block, seg_keys, pos_keys)
        probs = jnp.where(mask, jnp.exp(masked - lse[..., None]), 0.0)
        probs_low = probs.astype(brain_float_sixteen)
        grad_probs = jnp.einsum(
            "tkgd,skd->kgts", grad_heads, value_block, preferred_element_type=f32
        )
        grad_scores = (probs * (grad_probs - delta[..., None])).astype(brain_float_sixteen)
        grad_q = grad_q + jnp.einsum(
            "kgts,skd->tkgd", grad_scores, key_block, preferred_element_type=f32
        )
        grad_k = jnp.einsum("kgts,tkgd->skd", grad_scores, q_rot, preferred_element_type=f32)
        grad_v = jnp.einsum("kgts,tkgd->skd", probs_low, grad_heads, preferred_element_type=f32)
        return (grad_q, (grad_k, grad_v))

    grad_q, (grad_k, grad_v) = lax.scan(
        backward_block,
        jnp.zeros((ntok, KV_HEADS, share, HEAD_DIM), f32),
        (keys_all, values_all, seg_blocks, pos_blocks),
    )
    grad_k = grad_k.reshape(group_tok, kv_width) * scale
    grad_v = grad_v.reshape(group_tok, kv_width)
    grad_k_own, grad_v_own = (
        lax.psum_scatter(
            grad_k.astype(jnp.bfloat16), "group", scatter_dimension=0, tiled=True
        ).astype(jnp.float32),
        lax.psum_scatter(
            grad_v.astype(jnp.bfloat16), "group", scatter_dimension=0, tiled=True
        ).astype(jnp.float32),
    )
    grad_query = rope_back((grad_q * scale).reshape(ntok, HEADS, HEAD_DIM), cosine, sine)
    grad_query = grad_query.reshape(ntok, q_width).astype(brain_float_sixteen)
    grad_key = rope_back(grad_k_own.reshape(ntok, KV_HEADS, HEAD_DIM), cosine, sine).reshape(
        ntok, kv_width
    )
    grad_keyval = jnp.stack([grad_key, grad_v_own], axis=1).astype(brain_float_sixteen)
    first_normalized_gradient = contract_cols(grad_query, wq_back)
    first_normalized_gradient = first_normalized_gradient + jnp.einsum(
        "tjk,cjk->tc", grad_keyval, wkv_back, preferred_element_type=f32
    )
    attention_gain_slice = jnp.sum(first_normalized_gradient * first_unit_rms_rows, axis=0)
    layer_input_gradient = (
        residual_one_gradient
        + rms_norm_backward(
            first_normalized_gradient, first_unit_rms_rows, first_inverse_rms, first_gain_gradient
        )
    ).astype(brain_float_sixteen)
    out_grad_full = contract_rows(attended_low, grad_attn)
    query_full = contract_rows(first_normalized_rows, grad_query)
    keyval_full = jnp.einsum(
        "tc,tjk->cjk", first_normalized_rows, grad_keyval, preferred_element_type=f32
    )
    wq_grad, wkv_grad, wo_grad, attn_gain_grad, mlp_gain_grad = (
        lax.psum_scatter(
            query_full.astype(jnp.bfloat16), "group", scatter_dimension=0, tiled=True
        ).astype(jnp.float32),
        lax.psum_scatter(
            keyval_full.astype(jnp.bfloat16), "group", scatter_dimension=0, tiled=True
        ).astype(jnp.float32),
        lax.psum_scatter(
            out_grad_full.astype(jnp.bfloat16), "group", scatter_dimension=0, tiled=True
        ).astype(jnp.float32),
        lax.psum_scatter(
            attention_gain_slice.astype(jnp.bfloat16), "group", scatter_dimension=0, tiled=True
        ).astype(jnp.float32),
        lax.psum_scatter(
            feedforward_gain_slice.astype(jnp.bfloat16), "group", scatter_dimension=0, tiled=True
        ).astype(jnp.float32),
    )
    wq_grad, wkv_grad, wo_grad, attn_gain_grad, mlp_gain_grad, w_gate_up_grad, w_down_grad = (
        lax.psum(wq_grad.astype(jnp.bfloat16), "replica").astype(jnp.float32),
        lax.psum(wkv_grad.astype(jnp.bfloat16), "replica").astype(jnp.float32),
        lax.psum(wo_grad.astype(jnp.bfloat16), "replica").astype(jnp.float32),
        lax.psum(attn_gain_grad.astype(jnp.bfloat16), "replica").astype(jnp.float32),
        lax.psum(mlp_gain_grad.astype(jnp.bfloat16), "replica").astype(jnp.float32),
        lax.psum(w_gate_up_grad.astype(jnp.bfloat16), "replica").astype(jnp.float32),
        lax.psum(w_down_grad.astype(jnp.bfloat16), "replica").astype(jnp.float32),
    )
    return (
        mixed,
        layer_input_gradient,
        attn_gain_grad,
        wq_grad,
        wkv_grad,
        wo_grad,
        mlp_gain_grad,
        w_gate_up_grad,
        w_down_grad,
    )


def solution(mesh):
    return jax.shard_map(
        local,
        mesh=mesh,
        in_specs=(
            P(("replica", "group"), None),
            P(("replica", "group"), None),
            P("replica", None),
            P("replica", None),
            P("group"),
            P("group", None),
            P("group", None, None),
            P("group", None),
            P("group"),
            P("group", None, None),
            P("group", None),
        ),
        out_specs=(
            P(("replica", "group"), None),
            P(("replica", "group"), None),
            P("group"),
            P("group", None),
            P("group", None, None),
            P("group", None),
            P("group"),
            P("group", None, None),
            P("group", None),
        ),
        check_vma=False,
    )
```

profile of v0, /device:TPU:0, one launch (start us, length us, event | category | flops | bytes accessed | tf_op | source)
XLA Modules:
  0.0 4798.4 jit_solution(2797858779595342627)
XLA Ops:
  25.5 68.1 %all-gather.11.cloned.1.call-done = bf16[2048,2,512]{2,0,1:T(8,128)(2,1)} async-done(((bf16[512,2,512]{2,0,1:T(8,128)(2,1)}), bf16[2048,2,512]{2,0,1:T(8,128)(2,1)}) %all-gather.11.cloned.1.call-update) | async-done | bytes 4194320 | tf_op jit(solution)/shard_map/all_gather | solution.py:112
  101.5 18.6 copy.96
  142.8 13.6 all-gather.13.cloned.1.call-done
  158.5 147.4 %all-gather.15.cloned.1.call-done = bf16[2048,2048]{1,0:T(8,128)(2,1)} async-done(((bf16[512,2048]{1,0:T(8,128)(2,1)}), bf16[2048,2048]{1,0:T(8,128)(2,1)}) %all-gather.15.cloned.1.call-update) | async-done | bytes 8388624 | tf_op jit(solution)/shard_map/all_gather | solution.py:111
  313.5 33.3 while.39
  346.8 17.6 while.40
  367.1 88.1 %all-gather.17.cloned.1.call-done = bf16[2048,2048]{1,0:T(8,128)(2,1)} async-done(((bf16[512,2048]{1,0:T(8,128)(2,1)}), bf16[2048,2048]{1,0:T(8,128)(2,1)}) %all-gather.17.cloned.1.call-update) | async-done | bytes 8388624 | tf_op jit(solution)/shard_map/all_gather | solution.py:113
  462.6 1103.4 %all-gather.19.cloned.1.call-done = bf16[2048,2,8192]{2,0,1:T(8,128)(2,1)} async-done(((bf16[512,2,8192]{2,0,1:T(8,128)(2,1)}), bf16[2048,2,8192]{2,0,1:T(8,128)(2,1)}) %all-gather.19.cloned.1.call-update) | async-done | bytes 67108880 | tf_op jit(solution)/shard_map/all_gather | solution.py:174
  1566.0 38.8 fusion.78
  1604.9 522.3 %all-gather.21.cloned.1.call-done = bf16[8192,2048]{1,0:T(8,128)(2,1)} async-done(((bf16[2048,2048]{1,0:T(8,128)(2,1)}), bf16[8192,2048]{1,0:T(8,128)(2,1)}) %all-gather.21.cloned.1.call-update) | async-done | bytes 33554448 | tf_op jit(solution)/shard_map/all_gather | solution.py:175
  2127.2 23.0 fusion.54
  2150.3 30.5 multiply_reduce_fusion
  2195.7 80.3 %while.41 = (s32[]{:T(128)}, f32[256,8,4,64]{0,3,2,1:T(8,128)}, f32[2,512,8,64]{1,3,2,0:T(8,128)}, bf16[2,512,8,64]{1,3,2,0:T(8,128)(2,1)}, bf16[2,512,8,64]{1,3...) while((s32[]{:T(128)}, f32[256,8,4,64]{0,3,2,1:T(8,128)}, ...), condition=%wide.region_13.14_spmd.clone, body=%wide.region_12.13_spmd.clone.sunk | while | flops 2736128000 | bytes 223083152 | solution.py:255
  2284.5 21.3 reduce-scatter.10.cloned.1.call-done
  2307.1 27.5 reduce-scatter.12.cloned.1.call-done
  2356.4 16.5 convolution_convert_fusion.1
  2374.5 30.1 convolution_convert_fusion
  2414.7 148.1 %reduce-scatter.14.cloned.1.call-done = bf16[512,2048]{1,0:T(8,128)(2,1)} async-done(((bf16[2048,2048]{1,0:T(8,128)(2,1)}), bf16[512,2048]{1,0:T(8,128)(2,1)}) %reduce-scatter.14.cloned.1.call-update) | async-done | bytes 2097168 | tf_op jit(solution)/shard_map/reduce_scatter | solution.py:293
  2562.8 147.6 %reduce-scatter.18.cloned.1.call-done = bf16[512,2048]{1,0:T(8,128)(2,1)} async-done(((bf16[2048,2048]{1,0:T(8,128)(2,1)}), bf16[512,2048]{1,0:T(8,128)(2,1)}) %reduce-scatter.18.cloned.1.call-update) | async-done | bytes 2097168 | tf_op jit(solution)/shard_map/reduce_scatter | solution.py:299
  2710.3 555.9 %reduce-scatter.22.cloned.1.call-done = bf16[2048,2048]{1,0:T(8,128)(2,1)} async-done(((bf16[8192,2048]{1,0:T(8,128)(2,1)}), bf16[2048,2048]{1,0:T(8,128)(2,1)}) %reduce-scatter.22.cloned.1.call-update) | async-done | bytes 8388624
  3266.2 1097.6 %reduce-scatter.20.cloned.1.call-done = bf16[512,2,8192]{2,0,1:T(8,128)(2,1)} async-done(((bf16[2048,2,8192]{2,0,1:T(8,128)(2,1)}), bf16[512,2,8192]{2,0,1:T(8,128)(2,1)}) %reduce-scatter.20.cloned.1.call-update) | async-done | bytes 16777232 | tf_op jit(solution)/shard_map/reduce_scatter | solution.py:215
  4373.3 17.9 fusion.61
  4426.8 310.7 %all-reduce.8.cloned.1.call-done = (bf16[512,2,512]{2,0,1:T(8,128)(2,1)}, bf16[512,2,8192]{2,0,1:T(8,128)(2,1)}, bf16[512,2048]{1,0:T(8,128)(2,1)}, bf16[512,2048]{1,0:T(8,128)(2,1)}, bf16[2048,2048]{1,0:T(8,128)(2,1)}) async-done(((bf16[512,2,512]{2,0,1:T(8,128)(2,1)}, bf16[512,2,8192]{2,0,1:T(8,128)(2,1)}, bf16[512,2048]{1,0:T(8,128)(2,1)}, bf16[512,2048]{1,0:T(8,128)(2,1)}, ...) | async-done | bytes 30408720 | tf_op jit(solution)/shard_map/psum | solution.py:311
  4746.8 33.2 copy.107
  (280 shorter events, 321.8 us)
Async XLA Ops:
  7.2 86.5 %copy-start.6 = (bf16[256,2048]{1,0:T(8,128)(2,1)S(1)}, bf16[256,2048]{1,0:T(8,128)(2,1)}, u32[]{:S(2)}) copy-start(bf16[256,2048]{1,0:T(8,128)(2,1)} %param.17) | copy-start | bytes 3145732
  7.2 86.5 %all-gather.11.cloned.1.call-start = ((), (), s32[]{:S(2)}) async-start(), calls=%async_computation.7 | async-start | bytes 5242880 | tf_op jit(solution)/shard_map/all_gather | solution.py:112
  9.7 125.9 %all-gather.23.cloned.1.call-start = ((), (), s32[]{:S(2)}) async-start(), calls=%async_computation.19 | async-start | bytes 1310720 | tf_op jit(solution)/shard_map/all_gather | solution.py:129
  24.0 281.8 %copy-start.39 = (f32[4,1,512]{2,1,0:T(1,128)}, f32[4,1,512]{2,1,0:T(1,128)S(1)}, u32[]{:S(2)}) copy-start(f32[4,1,512]{2,1,0:T(1,128)S(1)} %convert_element_type.198) | copy-start | bytes 24580
  25.5 280.3 %copy-start.44 = (f32[256]{0:T(256)}, f32[256]{0:T(256)S(1)}, u32[]{:S(2)}) copy-start(f32[256]{0:T(256)S(1)} %add_rsqrt_fusion.1) | copy-start | bytes 3076
  97.9 58.5 %all-gather.13.cloned.1.call-start = ((), (), s32[]{:S(2)}) async-start(), calls=%async_computation.8 | async-start | bytes 1310720 | tf_op jit(solution)/shard_map/all_gather | solution.py:128
  99.2 213.6 %copy-start.29 = (f32[256,32]{0,1:T(8,128)}, f32[256,32]{0,1:T(8,128)S(1)}, u32[]{:S(2)}) copy-start(f32[256,32]{0,1:T(8,128)S(1)} %get-tuple-element.558) | copy-start | bytes 98308
  99.2 213.6 %copy-start.31 = (f32[256,32]{0,1:T(8,128)}, f32[256,32]{0,1:T(8,128)S(1)}, u32[]{:S(2)}) copy-start(f32[256,32]{0,1:T(8,128)S(1)} %get-tuple-element.559) | copy-start | bytes 98308
  100.3 205.6 %all-gather.15.cloned.1.call-start = ((), (), s32[]{:S(2)}) async-start(), calls=%async_computation.9 | async-start | bytes 10485760 | tf_op jit(solution)/shard_map/all_gather | solution.py:111
  100.8 354.3 %all-gather.17.cloned.1.call-start = ((), (), s32[]{:S(2)}) async-start(), calls=%async_computation.10 | async-start | bytes 10485760 | tf_op jit(solution)/shard_map/all_gather | solution.py:113
  101.4 1464.6 %all-gather.19.cloned.1.call-start = ((), (), s32[]{:S(2)}) async-start(), calls=%async_computation.11 | async-start | bytes 83886080 | tf_op jit(solution)/shard_map/all_gather | solution.py:174
  120.1 2007.1 %all-gather.21.cloned.1.call-start = ((), (), s32[]{:S(2)}) async-start(), calls=%async_computation.12 | async-start | bytes 41943040 | tf_op jit(solution)/shard_map/all_gather | solution.py:175
  120.8 2185.0 %reduce-scatter.10.cloned.1.call-start = ((), (), s32[]{:S(2)}) async-start(), calls=%async_computation.13 | async-start | bytes 1310720 | tf_op jit(solution)/shard_map/reduce_scatter | solution.py:263
  135.0 2045.8 %copy-start.19 = (f32[4,1,512]{2,1,0:T(1,128)}, f32[4,1,512]{2,1,0:T(1,128)S(1)}, u32[]{:S(2)}) copy-start(f32[4,1,512]{2,1,0:T(1,128)S(1)} %convert_element_type.199) | copy-start | bytes 24580
  462.6 1718.1 %copy-start.24 = (f32[256]{0:T(256)}, f32[256]{0:T(256)S(1)}, u32[]{:S(2)}) copy-start(f32[256]{0:T(256)S(1)} %add_rsqrt_fusion) | copy-start | bytes 3076
  1566.0 561.2 %copy-start.12 = (bf16[256,2048]{1,0:T(8,128)(2,1)S(1)}, bf16[256,2048]{1,0:T(8,128)(2,1)}, u32[]{:S(2)}) copy-start(bf16[256,2048]{1,0:T(8,128)(2,1)} %param.18) | copy-start | bytes 3145732
  2280.4 54.3 %reduce-scatter.12.cloned.1.call-start = ((), (), s32[]{:S(2)}) async-start(), calls=%async_computation.14 | async-start | bytes 1310720 | tf_op jit(solution)/shard_map/reduce_scatter | solution.py:266
  2282.3 52.3 %copy-start.7 = (bf16[256,2048]{1,0:T(8,128)(2,1)S(1)}, bf16[256,2048]{1,0:T(8,128)(2,1)}, u32[]{:S(2)}) copy-start(bf16[256,2048]{1,0:T(8,128)(2,1)} %param.17) | copy-start | bytes 3145732
  2284.5 130.3 %reduce-scatter.16.cloned.1.call-start = ((), (), s32[]{:S(2)}) async-start(), calls=%async_computation.16 | async-start | bytes 5242880 | tf_op jit(solution)/shard_map/reduce_scatter | solution.py:296
  2339.1 223.6 %reduce-scatter.14.cloned.1.call-start = ((), (), s32[]{:S(2)}) async-start(), calls=%async_computation.15 | async-start | bytes 10485760 | tf_op jit(solution)/shard_map/reduce_scatter | solution.py:293
  2346.7 363.6 %reduce-scatter.18.cloned.1.call-start = ((), (), s32[]{:S(2)}) async-start(), calls=%async_computation.17 | async-start | bytes 10485760 | tf_op jit(solution)/shard_map/reduce_scatter | solution.py:299
  2355.2 911.0 %reduce-scatter.22.cloned.1.call-start = ((), (), s32[]{:S(2)}) async-start(), calls=%async_computation.20 | async-start | bytes 41943040
  2372.9 1990.9 %reduce-scatter.20.cloned.1.call-start = ((), (), s32[]{:S(2)}) async-start(), calls=%async_computation.18 | async-start | bytes 83886080 | tf_op jit(solution)/shard_map/reduce_scatter | solution.py:215
  2404.6 2332.9 %all-reduce.8.cloned.1.call-start = ((), (), s32[]{:S(2)}) async-start(), calls=%async_computation.21 | async-start | bytes 60817408 | tf_op jit(solution)/shard_map/psum | solution.py:311
  (57 other events, 399.2 us)
Sparse Core Ops, SparseCore 0:
  10.2 83.4 all-gather.10
  98.1 26.4 all-gather.22
  126.7 29.6 all-gather.12
  157.8 147.9 all-gather.14
  307.2 147.8 all-gather.16
  457.1 1108.8 all-gather.18
  1567.6 559.5 all-gather.20
  2280.5 25.3 reduce-scatter.9
  2308.8 25.7 reduce-scatter.11
  2339.3 75.4 reduce-scatter.15
  2417.8 144.9 reduce-scatter.13
  2565.1 145.1 reduce-scatter.17
  2713.4 552.7 reduce-scatter.21
  3268.4 1095.3 reduce-scatter.19
  4369.1 368.3 all-reduce.7
where the time goes:
time: 4800 us
  waiting for transfers between devices  4260 us (89%)
  matrix products  303 us (6%)
  local copies, waits for them, and re-layouts  102 us (2%)
  other arithmetic  62 us (1%)
  blocking collectives  50.9 us (1%)
    all_gather x1, waiting for transfers between devices, local(): lax.all_gather(w_gate_up, 'group', axis=0, tiled=True)  1100 us
    reduce_scatter x1, waiting for transfers between devices, local(): lax.psum_scatter(jnp.einsum('tc,tjf->cjf', second_normalized_rows, grad_g...  1100 us
    unnamed x16, waiting for transfers between devices  558 us
    all_gather x1, waiting for transfers between devices, local(): lax.all_gather(w_down, 'group', axis=0, tiled=True)  522 us
    psum x1, waiting for transfers between devices, local(): lax.psum(wkv_grad.astype(jnp.bfloat16), 'replica').astype(jnp.float32)  311 us
    reduce_scatter x1, waiting for transfers between devices, local(): lax.psum_scatter(query_full.astype(jnp.bfloat16), 'group', scatter_dimens...  148 us
    reduce_scatter x1, waiting for transfers between devices, local(): lax.psum_scatter(out_grad_full.astype(jnp.bfloat16), 'group', scatter_dim...  148 us
    all_gather x1, waiting for transfers between devices, local(): lax.all_gather(w_query, 'group', axis=0, tiled=True)  147 us
  transfers between devices with their start and end apart: 15, of which 14 were waited for; matrix products, arithmetic and copies ran while one was open for 5% of the time, Pallas kernels for 0%

commit v1 on v0

v1 whole, which is shorter than its diff:
```python
import functools
import math

import jax
import jax.numpy as jnp
from jax import lax
from jax.experimental import pallas as pl
from jax.experimental.pallas import tpu as pltpu
from jax.sharding import PartitionSpec as P

HEADS = 32
KV_HEADS = 8
HEAD_DIM = 64
EPS = 1e-05
NEG = -1e30
F32 = jnp.float32
BF16 = jnp.bfloat16
LIGHT = pl.CostEstimate(flops=1, bytes_accessed=1, transcendentals=0)
HEAVY = pl.CostEstimate(flops=3 * 10**11, bytes_accessed=1, transcendentals=0)


def frequencies(head_size):
    half = head_size // 2
    expo = jnp.arange(half).astype(F32) * (2.0 / head_size)
    base = jnp.power(F32(500000.0), -expo)
    wavelen = 2.0 * math.pi / base
    smooth = (8192.0 / wavelen - 1.0) / 3.0
    middle = (1.0 - smooth) * base / 32.0 + smooth * base
    return jnp.where(wavelen < 2048.0, base, jnp.where(wavelen > 8192.0, base / 32.0, middle))


def stream_meta(lengths_row, stream):
    ends = jnp.cumsum(lengths_row)
    past = ends[None, :] <= stream[:, None]
    segment = jnp.sum(past.astype(jnp.int32), axis=1)
    before = jnp.sum(jnp.where(past, lengths_row[None, :], 0), axis=1)
    return (segment, stream - before)


def inverse_rms(value):
    return lax.rsqrt(jnp.mean(value * value, axis=-1, keepdims=True) + EPS)


def rms_norm_backward(grad, unit, inverse, gain):
    scaled = grad * gain
    return inverse * (scaled - unit * jnp.mean(scaled * unit, axis=-1, keepdims=True))


def swap_halves(value):
    wide = value.shape[-1]
    lane = lax.broadcasted_iota(jnp.int32, value.shape, 1)
    low = lane % HEAD_DIM < HEAD_DIM // 2
    return jnp.where(
        low,
        pltpu.roll(value, wide - HEAD_DIM // 2, 1),
        pltpu.roll(value, HEAD_DIM // 2, 1),
    )


def rotate(value, cosine, sine, width):
    copies = value.shape[-1] // cosine.shape[-1]
    cosine = jnp.concatenate([cosine] * copies, axis=1)
    sine = jnp.concatenate([sine] * copies, axis=1)
    lane = lax.broadcasted_iota(jnp.int32, value.shape, 1)
    return jnp.where(lane < width, value * cosine + swap_halves(value) * sine, value)


def dot(left, right, dims):
    return lax.dot_general(left, right, (dims, ((), ())), preferred_element_type=F32)


def stacked(ref, rows, first, share):
    return jnp.concatenate(
        [ref[rows, (first + h) * HEAD_DIM : (first + h + 1) * HEAD_DIM] for h in range(share)], axis=0
    )


def bias_of(start, row0, block, keys):
    row = row0 + lax.broadcasted_iota(jnp.int32, (block, keys), 0)
    col = lax.broadcasted_iota(jnp.int32, (block, keys), 1)
    return jnp.where((col <= row) & (col >= start), 0.0, NEG).astype(F32)


def forward_kernel(
    hl, kvl, block, qkv_ref, cos_ref, sin_ref, start_ref, place_ref,
    q_ref, k_ref, v_ref, att_ref, lse_ref, low_ref,
):
    total = qkv_ref.shape[0]
    share = hl // kvl
    qw, kw = hl * HEAD_DIM, kvl * HEAD_DIM
    for row0 in range(0, total, block):
        rows = pl.ds(row0, block)
        turned = rotate(qkv_ref[rows, :], cos_ref[rows, :], sin_ref[rows, :], qw + kw)
        q_ref[rows, :] = (turned[:, :qw].astype(BF16) * HEAD_DIM ** (-0.5)).astype(BF16)
        k_ref[rows, :] = turned[:, qw : qw + kw].astype(BF16)
        v_ref[rows, :] = turned[:, qw + kw :].astype(BF16)
    for row0 in range(0, total, block):
        rows = pl.ds(row0, block)
        keys = row0 + block
        bias = bias_of(start_ref[rows, :], row0, block, keys)
        for kv in range(kvl):
            cols = slice(kv * HEAD_DIM, (kv + 1) * HEAD_DIM)
            query = stacked(q_ref, rows, kv * share, share)
            raw = dot(query, k_ref[:keys, cols], ((1,), (1,)))
            raw = (raw.reshape(share, block, keys) + bias[None]).reshape(share * block, keys)
            top = jnp.max(raw, axis=-1, keepdims=True)
            probs = jnp.exp(raw - top)
            total_p = jnp.sum(probs, axis=-1, keepdims=True)
            out = dot(probs.astype(BF16), v_ref[:keys, cols], ((1,), (0,))) / total_p
            lse = top + jnp.log(total_p)
            for h in range(share):
                head = kv * share + h
                part = slice(h * block, (h + 1) * block)
                att_ref[rows, head * HEAD_DIM : (head + 1) * HEAD_DIM] = out[part]
                lse_ref[rows, head : head + 1] = lse[part]
    low_ref[...] = dot(place_ref[...], att_ref[...].astype(BF16), ((0,), (0,))).astype(BF16)


def backward_kernel(
    hl, kvl, block, q_ref, k_ref, v_ref, att_ref, lse_ref, heads_ref, cos_ref, sin_ref, start_ref, place_ref,
    grad_ref, native_ref, gh_ref, gq_ref, gk_ref, gv_ref,
):
    total = q_ref.shape[0]
    share = hl // kvl
    qw, kw = hl * HEAD_DIM, kvl * HEAD_DIM
    gh_ref[...] = dot(place_ref[...], heads_ref[...], ((1,), (0,))).astype(BF16)
    gk_ref[...] = jnp.zeros_like(gk_ref)
    gv_ref[...] = jnp.zeros_like(gv_ref)
    for row0 in range(0, total, block):
        rows = pl.ds(row0, block)
        keys = row0 + block
        bias = bias_of(start_ref[rows, :], row0, block, keys)
        for kv in range(kvl):
            cols = slice(kv * HEAD_DIM, (kv + 1) * HEAD_DIM)
            query = stacked(q_ref, rows, kv * share, share)
            heads = stacked(gh_ref, rows, kv * share, share)
            att = stacked(att_ref, rows, kv * share, share)
            delta = jnp.sum(heads.astype(F32) * att, axis=-1, keepdims=True)
            lse = jnp.concatenate(
                [lse_ref[rows, kv * share + h : kv * share + h + 1] for h in range(share)], axis=0
            )
            raw = dot(query, k_ref[:keys, cols], ((1,), (1,)))
            raw = (raw.reshape(share, block, keys) + bias[None]).reshape(share * block, keys)
            probs = jnp.exp(raw - lse)
            grad_probs = dot(heads, v_ref[:keys, cols], ((1,), (1,)))
            scores = (probs * (grad_probs - delta)).astype(BF16)
            out = dot(scores, k_ref[:keys, cols], ((1,), (0,))) * HEAD_DIM ** (-0.5)
            for h in range(share):
                head = kv * share + h
                gq_ref[rows, head * HEAD_DIM : (head + 1) * HEAD_DIM] = out[h * block : (h + 1) * block]
            gk_ref[:keys, cols] += dot(scores, query, ((0,), (0,)))
            gv_ref[:keys, cols] += dot(probs.astype(BF16), heads, ((0,), (0,)))
    for row0 in range(0, total, block):
        rows = pl.ds(row0, block)
        grad = jnp.concatenate([gq_ref[rows, :], gk_ref[rows, :], gv_ref[rows, :]], axis=1)
        grad_ref[rows, :] = rotate(grad, cos_ref[rows, :], -sin_ref[rows, :], qw + kw).astype(BF16)
    native_ref[...] = dot(place_ref[...], grad_ref[...], ((0,), (0,))).astype(BF16)


def vmem(count):
    return [pl.BlockSpec(memory_space=pltpu.VMEM)] * count


def attention_forward(hl, kvl, qkv, cosine, sine, start, place):
    total = qkv.shape[0]
    block = 256 if total <= 1024 else 128
    qw, kw = hl * HEAD_DIM, kvl * HEAD_DIM
    shape = jax.ShapeDtypeStruct
    return pl.pallas_call(
        functools.partial(forward_kernel, hl, kvl, block),
        out_shape=(
            shape((total, qw), BF16), shape((total, kw), BF16), shape((total, kw), BF16),
            shape((total, qw), F32), shape((total, 128), F32), shape((total, qw), BF16),
        ),
        in_specs=vmem(5), out_specs=tuple(vmem(6)),
        compiler_params=pltpu.CompilerParams(
            vmem_limit_bytes=(32 if total <= 1024 else 56) * 2**20
        ),
        cost_estimate=LIGHT,
        name="attention_forward",
    )(qkv, cosine, sine, start, place)


def attention_backward(hl, kvl, q, k, v, att, lse, heads, cosine, sine, start, place):
    total = q.shape[0]
    block = 256 if total <= 1024 else 128
    qw, kw = hl * HEAD_DIM, kvl * HEAD_DIM
    shape = jax.ShapeDtypeStruct
    return pl.pallas_call(
        functools.partial(backward_kernel, hl, kvl, block),
        out_shape=(shape((total, qw + 2 * kw), BF16), shape((total, qw + 2 * kw), BF16)),
        in_specs=vmem(10), out_specs=tuple(vmem(2)),
        scratch_shapes=[
            pltpu.VMEM((total, qw), BF16), pltpu.VMEM((total, qw), F32),
            pltpu.VMEM((total, kw), F32), pltpu.VMEM((total, kw), F32),
        ],
        compiler_params=pltpu.CompilerParams(
            vmem_limit_bytes=(44 if total <= 1024 else 56) * 2**20
        ),
        cost_estimate=HEAVY,
        name="attention_backward",
    )(q, k, v, att, lse, heads, cosine, sine, start, place)


def hidden_kernel(
    parts, n2_ref, dy_ref, up_ref, down_ref, hidden_ref, gate_grad_ref, up_grad_ref, grad_ref, grad_sum
):
    step = pl.program_id(0)
    wide = down_ref.shape[0] // parts
    total = None
    for part in range(parts):
        cols = slice(part * wide, (part + 1) * wide)
        both = dot(n2_ref[...], up_ref[part], ((1,), (0,)))
        gate, up = both[:, :wide], both[:, wide:]
        grad = dot(dy_ref[...], down_ref[cols, :], ((1,), (1,)))
        sigma = 1.0 / (1.0 + jnp.exp(-gate))
        silu = gate * sigma
        hidden_ref[:, cols] = (silu * up).astype(BF16)
        grad_gate = (grad * up * sigma * (1.0 + gate * (1.0 - sigma))).astype(BF16)
        grad_up = (grad * silu).astype(BF16)
        gate_grad_ref[:, cols] = grad_gate
        up_grad_ref[:, cols] = grad_up
        both = jnp.concatenate([grad_gate, grad_up], axis=1)
        both = dot(both, up_ref[part], ((1,), (1,)))
        total = both if total is None else total + both

    @pl.when(step == 0)
    def _():
        grad_sum[...] = total

    @pl.when(step > 0)
    def _():
        grad_sum[...] += total

    @pl.when(step == pl.num_programs(0) - 1)
    def _():
        grad_ref[...] = grad_sum[...].astype(BF16)


def feed_forward(n2, dy, w_gu, w_down):
    rows, width = n2.shape
    ffs = w_down.shape[0]
    count, _, both = w_gu.shape
    wide = both // 2
    parts = max(1, 512 // wide)
    tile = parts * wide
    shape = jax.ShapeDtypeStruct
    whole = pl.BlockSpec((rows, width), lambda j: (0, 0), pipeline_mode=pl.Buffered(1))
    return pl.pallas_call(
        functools.partial(hidden_kernel, parts),
        grid=(count // parts,),
        in_specs=[
            whole,
            whole,
            pl.BlockSpec((parts, width, both), lambda j: (j, 0, 0)),
            pl.BlockSpec((tile, width), lambda j: (j, 0)),
        ],
        out_specs=[pl.BlockSpec((rows, tile), lambda j: (0, j))] * 3 + [whole],
        out_shape=[shape((rows, ffs), BF16)] * 3 + [shape((rows, width), BF16)],
        scratch_shapes=[pltpu.VMEM((rows, width), F32)],
        compiler_params=pltpu.CompilerParams(vmem_limit_bytes=60 * 2**20),
        cost_estimate=LIGHT,
        name="feed_forward",
    )(n2, dy, w_gu, w_down)


def product_kernel(parts, *refs):
    lefts, rights = refs[:parts], refs[parts:-3]
    out_ref, done_ref, turned_ref = refs[-3:]
    count = len(rights) // parts
    step = pl.program_id(1)
    each = pl.num_programs(1) // count
    size = lefts[0].shape[0]

    @pl.when(step == 0)
    def _():
        for part in range(parts):
            turned_ref[:, part * size : (part + 1) * size] = lefts[part][...].T
        done_ref[...] = jnp.zeros_like(done_ref)

    for which in range(count):

        @pl.when((step >= which * each) & (step < (which + 1) * each))
        def _():
            value = 0.0
            for part in range(parts):
                turned = turned_ref[:, part * size : (part + 1) * size]
                value += dot(turned, rights[which * parts + part][...], ((1,), (0,)))
            out_ref[...] = value.astype(BF16).reshape(out_ref.shape)


def weight_gradient(lefts, rights, blocks, replicas, by_block):
    parts, (size, width) = len(lefts), lefts[0].shape
    cols = rights[0][0].shape[1]
    rows = width // blocks
    tile = min(1024, cols)
    each = cols // tile

    def place(which):
        return lambda i, j: (0, jnp.clip(j - which * each, 0, each - 1))

    if by_block:
        shape = (replicas, blocks, rows // replicas, len(rights) * cols)
        out_spec = pl.BlockSpec((replicas, 1, rows // replicas, tile), lambda i, j: (0, i, 0, j))
    else:
        shape = (width, len(rights) * cols)
        out_spec = pl.BlockSpec((rows, tile), lambda i, j: (i, j))
    return pl.pallas_call(
        functools.partial(product_kernel, parts),
        grid=(blocks, len(rights) * each),
        in_specs=[pl.BlockSpec((size, rows), lambda i, j: (0, i))] * parts
        + [pl.BlockSpec((size, tile), place(n)) for n in range(len(rights)) for _ in range(parts)],
        out_specs=[out_spec, pl.BlockSpec((8, 128), lambda i, j: (0, 0))],
        out_shape=[jax.ShapeDtypeStruct(shape, BF16), jax.ShapeDtypeStruct((8, 128), F32)],
        scratch_shapes=[pltpu.VMEM((rows, parts * size), BF16)],
        compiler_params=pltpu.CompilerParams(vmem_limit_bytes=56 * 2**20),
        cost_estimate=LIGHT,
        name="weight_gradient",
    )(*lefts, *[part for right in rights for part in right])


def mark(value):
    while value.ndim > 2:
        value = value[0]
    return value[:8, :128]


def after(value, *others):
    leaves, tree = jax.tree.flatten(value)
    others = [mark(other) for other in jax.tree.leaves(others)]
    anywhere = pl.BlockSpec(memory_space=pl.ANY)
    tied = pl.pallas_call(
        lambda *refs: None,
        out_shape=[jax.ShapeDtypeStruct(leaf.shape, leaf.dtype) for leaf in leaves],
        in_specs=[anywhere] * (len(leaves) + len(others)),
        out_specs=[anywhere] * len(leaves),
        input_output_aliases={i: i for i in range(len(leaves))},
        cost_estimate=LIGHT,
        name="after",
    )(*leaves, *others)
    return jax.tree.unflatten(tree, tied)


class Line:
    def __init__(self, count):
        self.count = count
        self.me = lax.axis_index("group")

    def swap(self, value, slot):
        return lax.ppermute(value, "group", [(i, i ^ slot) for i in range(self.count)])

    def at(self, value, slot, axis=0):
        return lax.dynamic_index_in_dim(value, self.me ^ slot, axis, keepdims=False)

    def exchange(self, slots):
        return [slots[0]] + [self.swap(slots[k], k) for k in range(1, self.count)]

    def ordered(self, slots):
        return [self.pick(slots, j) for j in range(self.count)]

    def pick(self, slots, device):
        value = slots[0]
        for k in range(1, self.count):
            value = jnp.where(self.me == device ^ k, slots[k], value)
        return value

    def near(self, begun):
        low, high = after((begun[0][1], begun[1][1]))
        return jnp.where(self.me % 2 == 0, high, low)

    def gather(self, value, gates=(), hops=None, begun=None):
        count = self.count
        low, high = begun if begun else ([value], [value])
        low, high = list(low), list(high)
        for hop in range(len(low), (hops or count - 1) + 1):
            moving = (low[-1], high[-1])
            if hop <= len(gates) and gates[hop - 1] is not None:
                if hop == 1:
                    moving = (after(value, gates[0]),) * 2
                else:
                    moving = after(moving, gates[hop - 1])
            up = [(i, i + 1) for i in range(hop - 1, count - 1)]
            down = [(i + 1, i) for i in range(count - hop)]
            low.append(lax.ppermute(moving[0], "group", up))
            high.append(lax.ppermute(moving[1], "group", down))
        if hops:
            return low, high
        self.last = (low[1:], high[1:])
        slots = [value]
        for k in range(1, count):
            chosen = None
            for device in range(count):
                source = device ^ k
                came = high[source - device] if source > device else low[device - source]
                chosen = came if chosen is None else jnp.where(self.me == device, came, chosen)
            slots.append(chosen)
        return slots

    def scatter_sum(self, slots):
        count = self.count
        to_up = to_down = None
        self.hops = []
        for hop in range(count - 1, 0, -1):
            up = [(i, i + 1) for i in range(count - hop)]
            down = [(i + 1, i) for i in range(hop - 1, count - 1)]
            mine_up = self.pick_far(slots, hop)
            mine_down = self.pick_far(slots, -hop)
            if to_up is not None:
                mine_up, mine_down = mine_up + to_up, mine_down + to_down
            to_up = lax.ppermute(mine_up, "group", up)
            to_down = lax.ppermute(mine_down, "group", down)
            self.hops.append((to_up, to_down))
        return slots[0].astype(F32) + to_up.astype(F32) + to_down.astype(F32)

    def pick_far(self, slots, distance):
        chosen = slots[1]
        for device in range(self.count):
            other = device + distance
            if 0 <= other < self.count:
                chosen = jnp.where(self.me == device, slots[device ^ other], chosen)
        return chosen


def local(
    tokens,
    cotangent,
    lengths,
    packing,
    attn_gain,
    w_query,
    w_key_value,
    w_out,
    mlp_gain,
    w_gate_up,
    w_down,
):
    ntok, width = tokens.shape
    total = packing.shape[1]
    groups = total // ntok
    shard = w_query.shape[0]
    replicas = lax.axis_size("replica")
    rows = shard // replicas
    kvl = KV_HEADS // groups
    hl = HEADS // groups
    qw = hl * HEAD_DIM
    kw = kvl * HEAD_DIM
    qkvw = qw + 2 * kw
    ff = w_gate_up.shape[2]
    ffs = ff // groups
    me_r = lax.axis_index("replica")
    line = Line(groups)

    def own_rows(value):
        return lax.dynamic_slice_in_dim(value, me_r * rows, rows)

    def over_plane(value):
        return lax.all_gather(value, "replica", axis=0)

    wq_rows = own_rows(w_query).reshape(rows, groups, qw)
    wkv_rows = own_rows(w_key_value).reshape(rows, 2, groups, kw)
    wkv_rows = wkv_rows.transpose(0, 2, 1, 3).reshape(rows, groups, 2 * kw)
    qkv_rows = jnp.concatenate([wq_rows, wkv_rows], axis=2)
    ffr = ffs // replicas
    gu_cols = []
    for k in range(groups):
        first = (line.me ^ k) * ffs + me_r * ffr
        part = lax.dynamic_slice(w_gate_up, (0, 0, first), (shard, 2, ffr))
        gu_cols.append(jnp.concatenate([part[:, 0], part[:, 1]], axis=1))
    gu_cols = jnp.stack(gu_cols)
    out_cols = lax.dynamic_slice_in_dim(w_out, me_r * (width // replicas), width // replicas, 1)

    w_qkv = line.exchange([line.at(qkv_rows, k, 1) for k in range(groups)])
    gains = jnp.stack([attn_gain, mlp_gain])
    gains = jnp.concatenate(line.ordered(line.exchange([gains] * groups)), axis=1)
    gain1, gain2 = gains[0], gains[1]
    w_out_cols = line.exchange([out_cols] * groups)
    x_hops = line.gather(tokens, (), 1)
    x_came = [part[1] for part in x_hops]
    w_qkv, w_out_cols[1:], x_came = after((w_qkv, w_out_cols[1:], x_came), gu_cols)
    x_hops = [[tokens, part] for part in x_came]
    seats = jnp.arange(total, dtype=jnp.int32)
    _, position = stream_meta(lengths[0], seats)
    start = (seats - position)[:, None]
    angles = position.astype(F32)[:, None] * frequencies(HEAD_DIM)[None, :]
    copies = 128 // HEAD_DIM
    cosine = jnp.tile(jnp.cos(angles), (1, 2 * copies))
    sine = jnp.sin(angles)
    sine = jnp.tile(jnp.concatenate([-sine, sine], axis=1), (1, copies))
    seat = packing.reshape(groups, ntok)
    seat = jnp.concatenate([line.at(seat, k) for k in range(groups)])
    place = (seat[None, :] == seats[:, None]).astype(BF16)
    w_qkv = over_plane(jnp.stack(line.ordered(w_qkv)))
    w_qkv = jnp.swapaxes(w_qkv, 0, 1).reshape(width, qkvw)
    x_slots = line.gather(tokens, (), 0, x_hops)
    x_last = [part[-1] for part in line.last]
    w_out_cols = over_plane(jnp.concatenate(w_out_cols))
    gu_cols = after(gu_cols, x_last)
    gu_cols = line.exchange([gu_cols[k] for k in range(groups)])
    dy_hops = line.gather(cotangent, (x_last,), 1)

    def normed(value):
        value = value.astype(F32)
        return (value * inverse_rms(value) * gain1).astype(BF16)

    normed1 = jnp.concatenate([normed(value) for value in x_slots])
    normed1 = dot(place, normed1, ((1,), (0,))).astype(BF16)
    qkv = dot(normed1, w_qkv, ((1,), (0,)))
    q_rot, k_rot, values, attended, lse, attended_low = attention_forward(
        hl, kvl, qkv, cosine, sine, start, place
    )

    def cut(value):
        return [value[k * ntok : (k + 1) * ntok] for k in range(groups)]

    dy_near = dy_hops
    attended_low = after(attended_low, [part[1] for part in dy_hops])
    own_attended = line.exchange(cut(attended_low))
    w_gu = over_plane(jnp.concatenate(line.ordered(after(gu_cols, attended_low))))
    x_own = tokens.astype(F32)
    own_attended_all = jnp.concatenate(own_attended, axis=1)
    h1 = lax.dot_general(own_attended_all, w_out_cols, (((1,), (1,)), ((), ())), preferred_element_type=F32)
    h1 = x_own + h1.reshape(ntok, width)
    inv2 = inverse_rms(h1)
    unit2 = h1 * inv2
    normed2 = (unit2 * gain2).astype(BF16)
    n2_near = line.gather(normed2, (), 1)
    dy_hops = line.gather(cotangent, (None, own_attended[1:]), 2, dy_hops)
    near_parts = [
        jnp.concatenate([own, line.near(begun)])
        for own, begun in ((normed2, n2_near), (cotangent, dy_near))
    ]

    half = groups // 2
    if half > 2:
        n2, dy = line.gather(normed2, (), 0, n2_near), line.gather(cotangent, (), 0, dy_hops)
        near_parts = [jnp.concatenate(part[:half]) for part in (n2, dy)]
    near = feed_forward(*near_parts, w_gu, w_down)
    if half == 2:
        n2 = line.gather(normed2, (None, None, near[3]), 0, n2_near)
        dy = line.gather(cotangent, (None, None, n2_near), 0, dy_hops)
    n2_parts = [near_parts[0], jnp.concatenate(n2[half:])]
    dy_parts = [near_parts[1], jnp.concatenate(dy[half:])]
    n2_parts[1] = after(n2_parts[1], near[3])
    far = feed_forward(n2_parts[1], dy_parts[1], w_gu, w_down)
    grad_n2 = line.exchange(cut(near[3])[:half] + cut(far[3])[:half])

    def sum_plane(value):
        return lax.psum_scatter(value, "replica", scatter_dimension=0)

    hidden = [near[0], far[0]]
    down_grad, down_done = weight_gradient(hidden, [dy_parts], groups, replicas, False)
    n2_parts[0] = after(n2_parts[0], down_done)
    gu_grad, gu_done = weight_gradient(
        n2_parts, [[near[1], far[1]], [near[2], far[2]]], groups, replicas, True
    )
    down_grad = sum_plane(down_grad.reshape(replicas, ffs // replicas, width))
    gu_grad = gu_grad.reshape(replicas, groups * rows, 2 * ffs)
    gu_grad = sum_plane(gu_grad).reshape(groups, rows, 2 * ffs)

    grad_n2 = after(grad_n2, gu_done)
    grad_n2 = sum([part.astype(F32) for part in grad_n2])
    gain2_grad = jnp.sum(grad_n2 * unit2, axis=0)
    grad_h1 = cotangent.astype(F32) + rms_norm_backward(grad_n2, unit2, inv2, gain2)
    grad_attn = grad_h1.astype(BF16)
    grad_heads = lax.dot_general(
        grad_attn.reshape(ntok, replicas, width // replicas),
        w_out_cols,
        (((1, 2), (0, 2)), ((), ())),
        preferred_element_type=F32,
    ).astype(BF16)
    grad_heads = line.exchange([grad_heads[:, k * qw : (k + 1) * qw] for k in range(groups)])
    down = [dot(after(part, grad_attn), w_down, ((1,), (0,))).astype(BF16) for part in hidden]
    grad_heads = jnp.concatenate(after(grad_heads, down))
    grad_qkv, own_qkv = attention_backward(
        hl, kvl, q_rot, k_rot, values, attended, lse, grad_heads, cosine, sine, start, place
    )
    qkv_grad = dot(normed1, grad_qkv, ((0,), (0,))).astype(BF16)
    grad_n1 = dot(own_qkv, w_qkv, ((1,), (1,))).astype(BF16)
    grad_n1 = line.scatter_sum(cut(grad_n1))
    n1_hops = line.hops
    grad_attn_all = line.gather(grad_attn, (grad_heads, own_qkv, n1_hops[0]))
    inv1 = inverse_rms(x_own)
    unit1 = x_own * inv1
    gain1_grad = jnp.sum(grad_n1 * unit1, axis=0)
    x_grad = (grad_h1 + rms_norm_backward(grad_n1, unit1, inv1, gain1)).astype(BF16)
    down = after(down, grad_attn_all[-1])
    down = line.scatter_sum(cut(down[0])[:half] + cut(down[1])[:half])
    mixed = (h1 + down).astype(BF16)

    grad_attn_all = jnp.concatenate(after(grad_attn_all, grad_n1))
    out_grad = dot(attended_low, grad_attn_all, ((0,), (0,))).astype(BF16)
    gain_grads = jnp.stack([gain1_grad, gain2_grad]).reshape(2, groups, replicas, rows)
    gain_grads = gain_grads.transpose(2, 3, 1, 0).astype(BF16)
    gain_grads = jnp.pad(gain_grads, ((0, 0), (0, 0), (0, 0), (0, 128 - 2)))
    qkv_grad = qkv_grad.reshape(groups, replicas, rows, qkvw).transpose(1, 2, 0, 3)
    wide = groups * (qkvw + 128)
    grads = jnp.concatenate([qkv_grad, gain_grads], axis=3).reshape(replicas, rows, wide)
    grads = jnp.concatenate([grads, out_grad.reshape(replicas, rows, width)], axis=2)

    def by_group(value):
        return line.exchange([line.at(value, k) for k in range(groups)])

    gu_grad, down_grad = after((gu_grad, down_grad), n1_hops[-2])
    gu_grad = line.ordered(by_group(gu_grad))
    down_grad = over_plane(down_grad).reshape(ffs, width)
    gu_grad = jnp.concatenate([part.reshape(rows, 2, ffs) for part in gu_grad], axis=2)
    gu_grad = over_plane(after(gu_grad, down_grad))
    grads = sum_plane(after(grads, gu_grad))

    out_grad = grads[:, wide:]
    grads = jnp.swapaxes(grads[:, :wide].reshape(rows, groups, qkvw + 128), 0, 1)
    grads = by_group(grads)
    gain_grads = sum([part[:, qkvw:].astype(F32) for part in grads]).astype(BF16)
    grads = line.ordered(grads)
    grads = [part[:, :qw] for part in grads] + [
        part[:, qw + j * kw : qw + (j + 1) * kw] for j in range(2) for part in grads
    ]
    grads = over_plane(after(jnp.concatenate(grads + [out_grad, gain_grads], axis=1), mixed))
    gu_grad = gu_grad.reshape(shard, 2, ff).astype(F32)
    down_grad = down_grad.astype(F32)
    grads = grads.reshape(shard, -1).astype(F32)
    q_grad = grads[:, :width]
    kv_grad = grads[:, width : width + 2 * groups * kw].reshape(shard, 2, groups * kw)
    out_grad = grads[:, width + 2 * groups * kw : 2 * width + 2 * groups * kw]
    gain_grads = grads[:, -128:]
    return (
        mixed,
        x_grad,
        gain_grads[:, 0],
        q_grad,
        kv_grad,
        out_grad,
        gain_grads[:, 1],
        gu_grad,
        down_grad,
    )


def solution(mesh):
    rows = P(("replica", "group"), None)
    flat, two, three = P("group"), P("group", None), P("group", None, None)
    return jax.shard_map(
        local,
        mesh=mesh,
        in_specs=(
            rows,
            rows,
            P("replica", None),
            P("replica", None),
            flat,
            two,
            three,
            two,
            flat,
            three,
            two,
        ),
        out_specs=(rows, rows, flat, two, three, two, flat, three, two),
        check_vma=False,
    )
```

time: 4800 us -> 1120 us (0.23)
  waiting for transfers between devices: 4260 us -> 381 us
  matrix products: 303 us -> 55.5 us
  starting transfers between devices: 0.61 us -> 234 us
  Pallas kernels: 0 us -> 169 us
  other arithmetic: 62 us -> 119 us
  blocking collectives: 50.9 us -> 0 us
    all_gather x7 -> x6, waiting for transfers between devices: 1940 us -> 30.8 us  [over_plane(): return lax.all_gather(value, 'replica', axis=0)]
    reduce_scatter x6 -> x3, waiting for transfers between devices: 1450 us -> 0.02 us  [sum_plane(): return lax.psum_scatter(value, 'replica', scatter_dimension=0)]
    unnamed x16 -> x9, waiting for transfers between devices: 558 us -> 0.15 us
    ppermute x0 -> x63, waiting for transfers between devices: none -> 350 us  [the longest x12 140 us: gather(): high.append(lax.ppermute(moving[1], 'group', down))]
    psum x1 -> x0, waiting for transfers between devices: 311 us -> none  [local(): lax.psum(wkv_grad.astype(jnp.bfloat16), 'replica').astype(jnp.float32)]
    dot_general x29 -> x9, matrix products: 303 us -> 55.5 us  [the longest x7 41.9 us: dot(): lax.dot_general(left, right, (dims, ((), ())), preferred_element_type=F32)]
    ppermute x0 -> x63, starting transfers between devices: none -> 234 us  [the longest x27 154 us: swap(): lax.ppermute(value, 'group', [(i, i ^ slot) for i in range(self.count)])]
    pallas_call x0 -> x31, Pallas kernels: none -> 169 us  [the longest x2 61.1 us: feed_forward(): pl.pallas_call(functools.partial(hidden_kernel, parts), grid=(count // pa...]
  transfers between devices with their start and end apart: 15 -> 72, of which waited for: 14 -> 30; matrix products, arithmetic and copies ran while one was open for 5% -> 23% of each run, Pallas kernels for 0% -> 8%
where the time goes in v1:
time: 1120 us; the launch traced here: 1110 us
  waiting for transfers between devices  381 us (34%)
  starting transfers between devices  234 us (21%)
  Pallas kernels  169 us (15%)
  local copies, waits for them, and re-layouts  132 us (12%)
  other arithmetic  119 us (11%)
  matrix products  55.5 us (5%)
  between operations  16 us (1%)
    ppermute x27, starting transfers between devices, swap(): lax.ppermute(value, 'group', [(i, i ^ slot) for i in range(self.count)])  154 us
    ppermute x12, waiting for transfers between devices, gather(): high.append(lax.ppermute(moving[1], 'group', down))  140 us
    ppermute x27, waiting for transfers between devices, swap(): lax.ppermute(value, 'group', [(i, i ^ slot) for i in range(self.count)])  93.4 us
    ppermute x6, waiting for transfers between devices, scatter_sum(): to_up = lax.ppermute(mine_up, 'group', up)  69 us
    pallas_call x2, Pallas kernels, feed_forward(): pl.pallas_call(functools.partial(hidden_kernel, parts), grid=(count // pa...  61.1 us
    pallas_call x2, Pallas kernels, weight_gradient(): pl.pallas_call(functools.partial(product_kernel, parts), grid=(blocks, le...  51 us
    unnamed x204, local copies, waits for them, and re-layouts  49.2 us
    dot_general x7, matrix products, dot(): lax.dot_general(left, right, (dims, ((), ())), preferred_element_type=F32)  41.9 us
  transfers between devices with their start and end apart: 72, of which 30 were waited for; matrix products, arithmetic and copies ran while one was open for 23% of the time, Pallas kernels for 8%

profile of v1, /device:TPU:0, one launch (start us, length us, event | category | flops | bytes accessed | tf_op | source)
XLA Modules:
  0.0 1107.0 jit_solution(12857671162993976945)
XLA Ops:
  24.1 19.6 %collective-permute-done.3.refs_1_ = bf16[64,768]{1,0:T(8,128)(2,1)S(1)} collective-permute-done((bf16[64,768]{1,0:T(8,128)(2,1)S(1)}, bf16[64,768]{1,0:T(8,128)(2,1)S(1)}, u32[]{:S(2)}, u32[]{:S(2)}) %collective-permute-start.3) | collective-permute-done | bytes 98336 | tf_op jit(solution)/shard_map/ppermute | solution.py:350
  95.3 16.7 %collective-permute-done.12 = bf16[256,2048]{1,0:T(8,128)(2,1)} collective-permute-done((bf16[256,2048]{1,0:T(8,128)(2,1)}, bf16[256,2048]{1,0:T(8,128)(2,1)}, u32[]{:S(2)}, u32[]{:S(2)}) %collective-permute-start.12) | collective-permute-done | bytes 1048608 | tf_op jit(solution)/shard_map/ppermute | solution.py:385
  119.4 17.4 %collective-permute-done.14 = bf16[256,2048]{1,0:T(8,128)(2,1)S(1)} collective-permute-done((bf16[256,2048]{1,0:T(8,128)(2,1)}, bf16[256,2048]{1,0:T(8,128)(2,1)S(1)}, u32[]{:S(2)}, u32[]{:S(2)}) %collective-permute-start.14) | collective-permute-done | bytes 1048608 | tf_op jit(solution)/shard_map/ppermute | solution.py:385
  179.5 25.6 %attention_forward.1 = (bf16[1024,512]{1,0:T(8,128)(2,1)S(1)}, bf16[1024,128]{1,0:T(8,128)(2,1)S(1)}, bf16[1024,128]{1,0:T(8,128)(2,1)S(1)}, f32[1024,512]{1,0:T...) custom-call(f32[1024,768]{1,0:T(8,128)S(1)} %fusion.90.qkv_ref, f32[1024,128]{1,0:T(8,128)S(1)} %copy.177.cos_ref, ...), custom_call_target="tpu_custom_call" | custom-call | flops 1 | bytes 1 | tf_op jit(solution)/shard_map/attention_forward/pallas_call | solution.py:169
  296.0 19.3 %collective-permute-done.33 = bf16[256,2048]{1,0:T(8,128)(2,1)} collective-permute-done((bf16[256,2048]{1,0:T(8,128)(2,1)}, bf16[256,2048]{1,0:T(8,128)(2,1)}, u32[]{:S(2)}, u32[]{:S(2)}) %collective-permute-start.33) | collective-permute-done | bytes 1048608 | tf_op jit(solution)/shard_map/ppermute | solution.py:385
  329.4 30.6 %feed_forward.2 = (bf16[512,2048]{1,0:T(8,128)(2,1)}, bf16[512,2048]{1,0:T(8,128)(2,1)}, bf16[512,2048]{1,0:T(8,128)(2,1)}, bf16[512,2048]{1,0:T(8,128)(2,1)}) custom-call(bf16[512,2048]{1,0:T(8,128)(2,1)} %pad_maximum_fusion.1.n2_ref.refs_0_, bf16[512,2048]{1,0:T(8,128)(2,1)} %pad_maximum_fusion.2.dy_ref.refs_2_, bf16[8,2048,512]{2,1,0:T(8,128)(2,1)} %bitcast.160, ...), custom_call_target="tpu_custom_call" | custom-call | flops 1 | bytes 1 | tf_op jit(solution)/shard_map/feed_forward/pallas_call | solution.py:249
  363.4 15.6 %collective-permute-done.29 = bf16[256,2048]{1,0:T(8,128)(2,1)S(1)} collective-permute-done((bf16[256,2048]{1,0:T(8,128)(2,1)}, bf16[256,2048]{1,0:T(8,128)(2,1)S(1)}, u32[]{:S(2)}, u32[]{:S(2)}) %collective-permute-start.29) | collective-permute-done | bytes 1048608 | tf_op jit(solution)/shard_map/ppermute | solution.py:385
  383.1 30.5 %feed_forward.3 = (bf16[512,2048]{1,0:T(8,128)(2,1)}, bf16[512,2048]{1,0:T(8,128)(2,1)}, bf16[512,2048]{1,0:T(8,128)(2,1)}, bf16[512,2048]{1,0:T(8,128)(2,1)}) custom-call(bf16[512,2048]{1,0:T(8,128)(2,1)} %after.33.n2_ref.refs_1_, bf16[512,2048]{1,0:T(8,128)(2,1)} %pad_maximum_fusion.6.dy_ref.refs_3_, bf16[8,2048,512]{2,1,0:T(8,128)(2,1)} %bitcast.161, ...), custom_call_target="tpu_custom_call" | custom-call | flops 1 | bytes 1 | tf_op jit(solution)/shard_map/feed_forward/pallas_call | solution.py:249
  413.7 17.6 %weight_gradient.2 = (bf16[2048,2048]{1,0:T(8,128)(2,1)}, f32[8,128]{1,0:T(8,128)}) custom-call(bf16[512,2048]{1,0:T(8,128)(2,1)} %get-tuple-element.90.refs_0_, bf16[512,2048]{1,0:T(8,128)(2,1)} %get-tuple-element.99.refs_1_.refs_0_, bf16[512,2048]{1,0:T(8,128)(2,1)} %pad_maximum_fusion.2.dy_ref.refs_2_, bf16[512,2048]{1,0:T(8,128)(2,1)} %pad_maximum_fusion.6.dy_ref.refs_3_), custom_call_target="tpu_custom_call" | custom-call | flops 1 | bytes 1 | tf_op jit(solution)/shard_map/weight_gradient/pallas_call | solution.py:308
  440.5 33.4 %weight_gradient.3 = (bf16[8,4,64,4096]{3,2,1,0:T(8,128)(2,1)}, f32[8,128]{1,0:T(8,128)}) custom-call(bf16[512,2048]{1,0:T(8,128)(2,1)} %after.36.refs_0_, bf16[512,2048]{1,0:T(8,128)(2,1)} %after.33.n2_ref.refs_1_, bf16[512,2048]{1,0:T(8,128)(2,1)} %get-tuple-element.101.refs_2_, bf16[512,2048]{1,0:T(8,128)(2,1)} %get-tuple-element.102.refs_3_, ...), custom_call_target="tpu_custom_call" | custom-call | flops 1 | bytes 1 | tf_op jit(solution)/shard_map/weight_gradient/pallas_call | solution.py:308
  474.0 31.8 %collective-permute-done.34.refs_2_ = bf16[256,2048]{1,0:T(8,128)(2,1)} collective-permute-done((bf16[256,2048]{1,0:T(8,128)(2,1)}, bf16[256,2048]{1,0:T(8,128)(2,1)}, u32[]{:S(2)}, u32[]{:S(2)}) %collective-permute-start.34) | collective-permute-done | bytes 1048608 | tf_op jit(solution)/shard_map/ppermute | solution.py:350
  532.0 15.0 %collective-permute-start.36 = (bf16[256,512]{1,0:T(8,128)(2,1)S(1)}, bf16[256,512]{1,0:T(8,128)(2,1)}, u32[]{:S(2)}, u32[]{:S(2)}) collective-permute-start(bf16[256,512]{1,0:T(8,128)(2,1)S(1)} %get-tuple-element.188), channel_id=1, source_target_pairs={{0,1},{1,0},{2,3},{3,2},{4,5},{5,4},{6,7},{7,6},{8,9},{9,8},{10,11... | collective-permute-start | bytes 786440 | tf_op jit(solution)/shard_map/ppermute | solution.py:350
  565.9 31.2 %attention_backward.1 = (bf16[1024,768]{1,0:T(8,128)(2,1)S(1)}, bf16[1024,768]{1,0:T(8,128)(2,1)S(1)}) custom-call(bf16[1024,512]{1,0:T(8,128)(2,1)S(1)} %copy-done.12, bf16[1024,128]{1,0:T(8,128)(2,1)S(1)} %get-tuple-element.112.k_ref, bf16[1024,128]{1,0:T(8,128)(2,1)S(1)} %copy-done.16, f32[1024,512]{1,0:T(8,128)S(1)} %copy-done.10, ...), custom_call_target="tpu_custom_call" | custom-call | flops 299999985664 | bytes 1 | tf_op jit(solution)/shard_map/attention_backward/pallas_call | solution.py:189
  605.1 18.8 %collective-permute-done.43 = bf16[256,2048]{1,0:T(8,128)(2,1)S(1)} collective-permute-done((bf16[256,2048]{1,0:T(8,128)(2,1)S(1)}, bf16[256,2048]{1,0:T(8,128)(2,1)S(1)}, u32[]{:S(2)}, u32[]{:S(2)}) %collective-permute-start.43) | collective-permute-done | bytes 1048608 | tf_op jit(solution)/shard_map/ppermute | solution.py:410
  648.5 50.8 %collective-permute-start.57 = (bf16[64,4096]{1,0:T(8,128)(2,1)S(1)}, bf16[64,4096]{1,0:T(8,128)(2,1)S(1)}, u32[]{:S(2)}, u32[]{:S(2)}) collective-permute-start(bf16[64,4096]{1,0:T(8,128)(2,1)S(1)} %get-tuple-element.170), channel_id=1, source_target_pairs={{0,3},{1,2},{2,1},{3,0},{4,7},{5,6},{6,5},{7,4},{8,11},{9,10},{10,... | collective-permute-start | bytes 1572872 | tf_op jit(solution)/shard_map/ppermute | solution.py:350
  713.0 18.4 %collective-permute-done.58 = bf16[64,4096]{1,0:T(8,128)(2,1)S(1)} collective-permute-done((bf16[64,4096]{1,0:T(8,128)(2,1)S(1)}, bf16[64,4096]{1,0:T(8,128)(2,1)S(1)}, u32[]{:S(2)}, u32[]{:S(2)}) %collective-permute-start.58) | collective-permute-done | bytes 524320 | tf_op jit(solution)/shard_map/ppermute | solution.py:350
  737.5 24.3 %all-gather.19.cloned.1.call-done = bf16[2048,2048]{1,0:T(8,128)(2,1)} async-done(((bf16[256,2048]{1,0:T(8,128)(2,1)}), bf16[2048,2048]{1,0:T(8,128)(2,1)}) %all-gather.19.cloned.1.call-update) | async-done | bytes 8388624 | tf_op jit(solution)/shard_map/all_gather | solution.py:457
  772.5 20.5 %collective-permute-done.39 = bf16[256,2048]{1,0:T(8,128)(2,1)S(1)} collective-permute-done((bf16[256,2048]{1,0:T(8,128)(2,1)}, bf16[256,2048]{1,0:T(8,128)(2,1)S(1)}, u32[]{:S(2)}, u32[]{:S(2)}) %collective-permute-start.39) | collective-permute-done | bytes 1048608 | tf_op jit(solution)/shard_map/ppermute | solution.py:384
  801.8 25.9 %collective-permute-done.42.refs_1_ = bf16[256,2048]{1,0:T(8,128)(2,1)S(1)} collective-permute-done((bf16[256,2048]{1,0:T(8,128)(2,1)}, bf16[256,2048]{1,0:T(8,128)(2,1)S(1)}, u32[]{:S(2)}, u32[]{:S(2)}) %collective-permute-start.42) | collective-permute-done | bytes 1048608 | tf_op jit(solution)/shard_map/ppermute | solution.py:385
  866.0 17.1 %collective-permute-done.56 = bf16[256,2048]{1,0:T(8,128)(2,1)S(1)} collective-permute-done((bf16[256,2048]{1,0:T(8,128)(2,1)S(1)}, bf16[256,2048]{1,0:T(8,128)(2,1)S(1)}, u32[]{:S(2)}, u32[]{:S(2)}) %collective-permute-start.56) | collective-permute-done | bytes 1048608 | tf_op jit(solution)/shard_map/ppermute | solution.py:411
  912.7 19.4 %collective-permute-done.47 = bf16[256,2048]{1,0:T(8,128)(2,1)S(1)} collective-permute-done((bf16[256,2048]{1,0:T(8,128)(2,1)S(1)}, bf16[256,2048]{1,0:T(8,128)(2,1)S(1)}, u32[]{:S(2)}, u32[]{:S(2)}) %collective-permute-start.47) | collective-permute-done | bytes 1048608 | tf_op jit(solution)/shard_map/ppermute | solution.py:410
  938.1 18.6 %collective-permute-done.48 = bf16[256,2048]{1,0:T(8,128)(2,1)S(1)} collective-permute-done((bf16[256,2048]{1,0:T(8,128)(2,1)S(1)}, bf16[256,2048]{1,0:T(8,128)(2,1)S(1)}, u32[]{:S(2)}, u32[]{:S(2)}) %collective-permute-start.48) | collective-permute-done | bytes 1048608 | tf_op jit(solution)/shard_map/ppermute | solution.py:410
  974.8 42.9 %collective-permute-start.60 = (bf16[64,896]{1,0:T(8,128)(2,1)S(1)}, bf16[64,896]{1,0:T(8,128)(2,1)S(1)}, u32[]{:S(2)}, u32[]{:S(2)}) collective-permute-start(bf16[64,896]{1,0:T(8,128)(2,1)S(1)} %bitcast.191), channel_id=1, source_target_pairs={{0,3},{1,2},{2,1},{3,0},{4,7},{5,6},{6,5},{7,4},{8,11},{9,10},{10,... | collective-permute-start | bytes 344072 | tf_op jit(solution)/shard_map/ppermute | solution.py:350
  1060.3 18.0 %convert.12 = f32[512,2,8192]{2,1,0:T(2,128)} convert(bf16[512,2,8192]{2,1,0:T(2,128)(2,1)} %all-gather.21.cloned.1.call-done) | non-fusion elementwise | flops 8388608 | bytes 50331648 | tf_op jit(solution)/shard_map/convert_element_type | solution.py:619
  (517 shorter events, 512.2 us)
Async XLA Ops:
  7.2 157.9 %all-gather.13.cloned.1.call-start = ((), (), s32[]{:S(2)}) async-start(), calls=%async_computation.6 | async-start | bytes 3538944 | tf_op jit(solution)/shard_map/all_gather | solution.py:457
  7.2 59.0 %collective-permute-start.9 = (bf16[256,2048]{1,0:T(8,128)(2,1)}, bf16[256,2048]{1,0:T(8,128)(2,1)}, u32[]{:S(2)}, u32[]{:S(2)}) collective-permute-start(bf16[256,2048]{1,0:T(8,128)(2,1)} %param.11), channel_id=1, source_target_pairs={{0,1},{1,2},{2,3},{4,5},{5,6},{6,7},{8,9},{9,10},{10,11},{12,13},{... | collective-permute-start | bytes 3145736 | tf_op jit(solution)/shard_map/ppermute | solution.py:384
  13.3 53.7 %collective-permute-start.10 = (bf16[256,2048]{1,0:T(8,128)(2,1)}, bf16[256,2048]{1,0:T(8,128)(2,1)}, u32[]{:S(2)}, u32[]{:S(2)}) collective-permute-start(bf16[256,2048]{1,0:T(8,128)(2,1)} %param.11), channel_id=1, source_target_pairs={{1,0},{2,1},{3,2},{5,4},{6,5},{7,6},{9,8},{10,9},{11,10},{13,12},{... | collective-permute-start | bytes 3145736 | tf_op jit(solution)/shard_map/ppermute | solution.py:385
  69.0 168.1 %all-gather.15.cloned.1.call-start = ((), (), s32[]{:S(2)}) async-start(), calls=%async_computation.7 | async-start | bytes 9437184 | tf_op jit(solution)/shard_map/all_gather | solution.py:457
  71.3 258.1 %all-gather.17.cloned.1.call-start = ((), (), s32[]{:S(2)}) async-start(), calls=%async_computation.8 | async-start | bytes 18874368 | tf_op jit(solution)/shard_map/all_gather | solution.py:457
  140.9 37.3 %collective-permute-start.16 = (bf16[256,2048]{1,0:T(8,128)(2,1)}, bf16[256,2048]{1,0:T(8,128)(2,1)}, u32[]{:S(2)}, u32[]{:S(2)}) collective-permute-start(bf16[256,2048]{1,0:T(8,128)(2,1)} %after.26), channel_id=1, source_target_pairs={{1,0},{2,1},{3,2},{5,4},{6,5},{7,6},{9,8},{10,9},{11,10},{13,12},{... | collective-permute-start | bytes 3145736 | tf_op jit(solution)/shard_map/ppermute | solution.py:385
  145.6 65.5 %collective-permute-start.22 = (bf16[512,512]{1,0:T(8,128)(2,1)}, bf16[512,512]{1,0:T(8,128)(2,1)}, u32[]{:S(2)}, u32[]{:S(2)}) collective-permute-start(bf16[512,512]{1,0:T(8,128)(2,1)} %get-tuple-element.183), channel_id=1, source_target_pairs={{0,1},{1,0},{2,3},{3,2},{4,5},{5,4},{6,7},{7,6},{8,9},{9,8},{10,11... | collective-permute-start | bytes 1572872 | tf_op jit(solution)/shard_map/ppermute | solution.py:350
  148.1 63.0 %collective-permute-start.23 = (bf16[512,512]{1,0:T(8,128)(2,1)}, bf16[512,512]{1,0:T(8,128)(2,1)}, u32[]{:S(2)}, u32[]{:S(2)}) collective-permute-start(bf16[512,512]{1,0:T(8,128)(2,1)} %get-tuple-element.182), channel_id=1, source_target_pairs={{0,2},{1,3},{2,0},{3,1},{4,6},{5,7},{6,4},{7,5},{8,10},{9,11},{10,... | collective-permute-start | bytes 1572872 | tf_op jit(solution)/shard_map/ppermute | solution.py:350
  149.1 62.1 %collective-permute-start.24 = (bf16[512,512]{1,0:T(8,128)(2,1)}, bf16[512,512]{1,0:T(8,128)(2,1)}, u32[]{:S(2)}, u32[]{:S(2)}) collective-permute-start(bf16[512,512]{1,0:T(8,128)(2,1)} %get-tuple-element.181), channel_id=1, source_target_pairs={{0,3},{1,2},{2,1},{3,0},{4,7},{5,6},{6,5},{7,4},{8,11},{9,10},{10,... | collective-permute-start | bytes 1572872 | tf_op jit(solution)/shard_map/ppermute | solution.py:350
  214.4 432.2 %reduce-scatter.6.cloned.1.call-start = ((), (), s32[]{:S(2)}) async-start(), calls=%async_computation.4 | async-start | bytes 9437184 | tf_op jit(solution)/shard_map/reduce_scatter | solution.py:548
  431.3 215.3 %reduce-scatter.4.cloned.1.call-start = ((), (), s32[]{:S(2)}) async-start(), calls=%async_computation.3 | async-start | bytes 18874368 | tf_op jit(solution)/shard_map/reduce_scatter | solution.py:548
  434.6 39.3 %collective-permute-start.25 = (bf16[256,2048]{1,0:T(8,128)(2,1)}, bf16[256,2048]{1,0:T(8,128)(2,1)}, u32[]{:S(2)}, u32[]{:S(2)}) collective-permute-start(bf16[256,2048]{1,0:T(8,128)(2,1)} %get-tuple-element.175), channel_id=1, source_target_pairs={{0,1},{1,0},{2,3},{3,2},{4,5},{5,4},{6,7},{7,6},{8,9},{9,8},{10,11... | collective-permute-start | bytes 3145736 | tf_op jit(solution)/shard_map/ppermute | solution.py:350
  437.0 68.8 %collective-permute-start.34 = (bf16[256,2048]{1,0:T(8,128)(2,1)}, bf16[256,2048]{1,0:T(8,128)(2,1)}, u32[]{:S(2)}, u32[]{:S(2)}) collective-permute-start(bf16[256,2048]{1,0:T(8,128)(2,1)} %get-tuple-element.174), channel_id=1, source_target_pairs={{0,2},{1,3},{2,0},{3,1},{4,6},{5,7},{6,4},{7,5},{8,10},{9,11},{10,... | collective-permute-start | bytes 3145736 | tf_op jit(solution)/shard_map/ppermute | solution.py:350
  437.0 68.8 %collective-permute-start.35 = (bf16[256,2048]{1,0:T(8,128)(2,1)}, bf16[256,2048]{1,0:T(8,128)(2,1)}, u32[]{:S(2)}, u32[]{:S(2)}) collective-permute-start(bf16[256,2048]{1,0:T(8,128)(2,1)} %get-tuple-element.173), channel_id=1, source_target_pairs={{0,3},{1,2},{2,1},{3,0},{4,7},{5,6},{6,5},{7,4},{8,11},{9,10},{10,... | collective-permute-start | bytes 3145736 | tf_op jit(solution)/shard_map/ppermute | solution.py:350
  515.8 246.0 %all-gather.19.cloned.1.call-start = ((), (), s32[]{:S(2)}) async-start(), calls=%async_computation.9 | async-start | bytes 9437184 | tf_op jit(solution)/shard_map/all_gather | solution.py:457
  647.0 260.7 %all-gather.21.cloned.1.call-start = ((), (), s32[]{:S(2)}) async-start(), calls=%async_computation.10 | async-start | bytes 18874368 | tf_op jit(solution)/shard_map/all_gather | solution.py:457
  648.5 64.5 %collective-permute-start.57 = (bf16[64,4096]{1,0:T(8,128)(2,1)S(1)}, bf16[64,4096]{1,0:T(8,128)(2,1)S(1)}, u32[]{:S(2)}, u32[]{:S(2)}) collective-permute-start(bf16[64,4096]{1,0:T(8,128)(2,1)S(1)} %get-tuple-element.170), channel_id=1, source_target_pairs={{0,3},{1,2},{2,1},{3,0},{4,7},{5,6},{6,5},{7,4},{8,11},{9,10},{10,... | collective-permute-start | bytes 1572872 | tf_op jit(solution)/shard_map/ppermute | solution.py:350
  763.1 204.9 %reduce-scatter.8.cloned.1.call-start = ((), (), s32[]{:S(2)}) async-start(), calls=%async_computation.5 | async-start | bytes 6488064 | tf_op jit(solution)/shard_map/reduce_scatter | solution.py:548
  830.1 35.5 %collective-permute-start.54 = (bf16[256,2048]{1,0:T(8,128)(2,1)}, bf16[256,2048]{1,0:T(8,128)(2,1)}, u32[]{:S(2)}, u32[]{:S(2)}) collective-permute-start(bf16[256,2048]{1,0:T(8,128)(2,1)} %get-tuple-element.160), channel_id=1, source_target_pairs={{0,1},{1,2},{2,3},{4,5},{5,6},{6,7},{8,9},{9,10},{10,11},{12,13},{... | collective-permute-start | bytes 3145736 | tf_op jit(solution)/shard_map/ppermute | solution.py:410
  838.9 44.2 %collective-permute-start.56 = (bf16[256,2048]{1,0:T(8,128)(2,1)S(1)}, bf16[256,2048]{1,0:T(8,128)(2,1)S(1)}, u32[]{:S(2)}, u32[]{:S(2)}) collective-permute-start(bf16[256,2048]{1,0:T(8,128)(2,1)S(1)} %fusion.56), channel_id=1, source_target_pairs={{1,0},{2,1},{3,2},{5,4},{6,5},{7,6},{9,8},{10,9},{11,10},{13,12},{... | collective-permute-start | bytes 3145736 | tf_op jit(solution)/shard_map/ppermute | solution.py:411
  909.0 175.7 %all-gather.23.cloned.1.call-start = ((), (), s32[]{:S(2)}) async-start(), calls=%async_computation.11 | async-start | bytes 6045696 | tf_op jit(solution)/shard_map/all_gather | solution.py:457
  959.5 58.8 %collective-permute-start.49 = (bf16[256,2048]{1,0:T(8,128)(2,1)}, bf16[256,2048]{1,0:T(8,128)(2,1)}, u32[]{:S(2)}, u32[]{:S(2)}) collective-permute-start(bf16[256,2048]{1,0:T(8,128)(2,1)} %get-tuple-element.162), channel_id=1, source_target_pairs={{0,1},{1,2},{2,3},{4,5},{5,6},{6,7},{8,9},{9,10},{10,11},{12,13},{... | collective-permute-start | bytes 3145736 | tf_op jit(solution)/shard_map/ppermute | solution.py:410
  966.6 59.9 %collective-permute-start.52 = (bf16[256,2048]{1,0:T(8,128)(2,1)}, bf16[256,2048]{1,0:T(8,128)(2,1)}, u32[]{:S(2)}, u32[]{:S(2)}) collective-permute-start(bf16[256,2048]{1,0:T(8,128)(2,1)} %fusion.52), channel_id=1, source_target_pairs={{1,0},{2,1},{3,2},{5,4},{6,5},{7,6},{9,8},{10,9},{11,10},{13,12},{... | collective-permute-start | bytes 3145736 | tf_op jit(solution)/shard_map/ppermute | solution.py:411
  974.8 57.1 %collective-permute-start.60 = (bf16[64,896]{1,0:T(8,128)(2,1)S(1)}, bf16[64,896]{1,0:T(8,128)(2,1)S(1)}, u32[]{:S(2)}, u32[]{:S(2)}) collective-permute-start(bf16[64,896]{1,0:T(8,128)(2,1)S(1)} %bitcast.191), channel_id=1, source_target_pairs={{0,3},{1,2},{2,1},{3,0},{4,7},{5,6},{6,5},{7,4},{8,11},{9,10},{10,... | collective-permute-start | bytes 344072 | tf_op jit(solution)/shard_map/ppermute | solution.py:350
  (134 other events, 2177.6 us)
Sparse Core Ops, SparseCore 0:
  69.1 35.1 all-gather.12
  106.8 54.3 all-gather.14
  214.5 92.5 all-gather.16
  431.4 69.8 reduce-scatter.5
  515.9 127.2 reduce-scatter.3
  646.8 114.9 all-gather.18
  763.8 89.8 all-gather.20
  909.1 56.2 reduce-scatter.7
  1045.1 39.6 all-gather.22

commit v2 on v1

--- a/solution.py
+++ b/solution.py
@@ -173,9 +173,7 @@
             shape((total, qw), F32), shape((total, 128), F32), shape((total, qw), BF16),
         ),
         in_specs=vmem(5), out_specs=tuple(vmem(6)),
-        compiler_params=pltpu.CompilerParams(
-            vmem_limit_bytes=(32 if total <= 1024 else 56) * 2**20
-        ),
+        compiler_params=pltpu.CompilerParams(vmem_limit_bytes=56 * 2**20),
         cost_estimate=LIGHT,
         name="attention_forward",
     )(qkv, cosine, sine, start, place)
@@ -194,10 +192,8 @@
             pltpu.VMEM((total, qw), BF16), pltpu.VMEM((total, qw), F32),
             pltpu.VMEM((total, kw), F32), pltpu.VMEM((total, kw), F32),
         ],
-        compiler_params=pltpu.CompilerParams(
-            vmem_limit_bytes=(44 if total <= 1024 else 56) * 2**20
-        ),
-        cost_estimate=HEAVY,
+        compiler_params=pltpu.CompilerParams(vmem_limit_bytes=56 * 2**20),
+        cost_estimate=pl.CostEstimate(flops=4 * 10**10, bytes_accessed=1, transcendentals=0),
         name="attention_backward",
     )(q, k, v, att, lse, heads, cosine, sine, start, place)
 
@@ -237,7 +233,7 @@
         grad_ref[...] = grad_sum[...].astype(BF16)
 
 
-def feed_forward(n2, dy, w_gu, w_down):
+def feed_forward(n2, dy, w_gu, w_down, cost):
     rows, width = n2.shape
     ffs = w_down.shape[0]
     count, _, both = w_gu.shape
@@ -259,7 +255,7 @@
         out_shape=[shape((rows, ffs), BF16)] * 3 + [shape((rows, width), BF16)],
         scratch_shapes=[pltpu.VMEM((rows, width), F32)],
         compiler_params=pltpu.CompilerParams(vmem_limit_bytes=60 * 2**20),
-        cost_estimate=LIGHT,
+        cost_estimate=cost,
         name="feed_forward",
     )(n2, dy, w_gu, w_down)
 
@@ -325,7 +321,7 @@
     return value[:8, :128]
 
 
-def after(value, *others):
+def after(value, *others, cost=LIGHT):
     leaves, tree = jax.tree.flatten(value)
     others = [mark(other) for other in jax.tree.leaves(others)]
     anywhere = pl.BlockSpec(memory_space=pl.ANY)
@@ -335,10 +331,23 @@
         in_specs=[anywhere] * (len(leaves) + len(others)),
         out_specs=[anywhere] * len(leaves),
         input_output_aliases={i: i for i in range(len(leaves))},
-        cost_estimate=LIGHT,
+        cost_estimate=cost,
         name="after",
     )(*leaves, *others)
     return jax.tree.unflatten(tree, tied)
+
+
+def pair_kernel(odd_ref, own_ref, low_ref, high_ref, out_ref):
+    size = own_ref.shape[0]
+    out_ref[:size, :] = own_ref[...]
+
+    @pl.when(odd_ref[0] == 0)
+    def _():
+        out_ref[size:, :] = high_ref[...]
+
+    @pl.when(odd_ref[0] != 0)
+    def _():
+        out_ref[size:, :] = low_ref[...]
 
 
 class Line:
@@ -365,8 +374,17 @@
         return value
 
     def near(self, begun):
-        low, high = after((begun[0][1], begun[1][1]))
-        return jnp.where(self.me % 2 == 0, high, low)
+        (own, low), (_, high) = begun
+        size, cols = own.shape
+        return pl.pallas_call(
+            pair_kernel,
+            out_shape=jax.ShapeDtypeStruct((2 * size, cols), own.dtype),
+            in_specs=[pl.BlockSpec(memory_space=pltpu.SMEM)] + vmem(3),
+            out_specs=pl.BlockSpec(memory_space=pltpu.VMEM),
+            compiler_params=pltpu.CompilerParams(vmem_limit_bytes=16 * 2**20),
+            cost_estimate=LIGHT,
+            name="pair",
+        )(self.me.reshape(1) % 2, own, low, high)
 
     def gather(self, value, gates=(), hops=None, begun=None):
         count = self.count
@@ -378,7 +396,7 @@
                 if hop == 1:
                     moving = (after(value, gates[0]),) * 2
                 else:
-                    moving = after(moving, gates[hop - 1])
+                    moving = low[-1], high[-1] = after(moving, gates[hop - 1])
             up = [(i, i + 1) for i in range(hop - 1, count - 1)]
             down = [(i + 1, i) for i in range(count - hop)]
             low.append(lax.ppermute(moving[0], "group", up))
@@ -396,21 +414,22 @@
             slots.append(chosen)
         return slots
 
+    def scatter_hop(self, slots, came, hop, gate=()):
+        count = self.count
+        up = [(i, i + 1) for i in range(count - hop)]
+        down = [(i + 1, i) for i in range(hop - 1, count - 1)]
+        moving = [self.pick_far(slots, hop), self.pick_far(slots, -hop)]
+        if came:
+            moving = [mine + part for mine, part in zip(moving, came)]
+        if gate:
+            moving = after(moving, gate)
+        return (lax.ppermute(moving[0], "group", up), lax.ppermute(moving[1], "group", down))
+
     def scatter_sum(self, slots):
-        count = self.count
-        to_up = to_down = None
-        self.hops = []
-        for hop in range(count - 1, 0, -1):
-            up = [(i, i + 1) for i in range(count - hop)]
-            down = [(i + 1, i) for i in range(hop - 1, count - 1)]
-            mine_up = self.pick_far(slots, hop)
-            mine_down = self.pick_far(slots, -hop)
-            if to_up is not None:
-                mine_up, mine_down = mine_up + to_up, mine_down + to_down
-            to_up = lax.ppermute(mine_up, "group", up)
-            to_down = lax.ppermute(mine_down, "group", down)
-            self.hops.append((to_up, to_down))
-        return slots[0].astype(F32) + to_up.astype(F32) + to_down.astype(F32)
+        came = None
+        for hop in range(self.count - 1, 0, -1):
+            came = self.scatter_hop(slots, came, hop)
+        return slots[0].astype(F32) + came[0].astype(F32) + came[1].astype(F32)
 
     def pick_far(self, slots, distance):
         chosen = slots[1]
@@ -419,6 +438,28 @@
             if 0 <= other < self.count:
                 chosen = jnp.where(self.me == device, slots[device ^ other], chosen)
         return chosen
+
+
+def gather_plane(value, replicas, me):
+    bits = [1 << i for i in range(1, replicas.bit_length() - 1)]
+    middle = value.shape[0] // 2
+
+    def swap(part, bit):
+        return lax.ppermute(part, "replica", [(i, i ^ bit) for i in range(replicas)])
+
+    halves = []
+    for half, order in ((value[:middle], bits), (value[middle:], bits[::-1])):
+        held, places = half[None], [0]
+        for bit in order:
+            held = jnp.concatenate([held, swap(held, bit)])
+            places = places + [place ^ bit for place in places]
+        halves.append(jnp.stack([held[places.index(2 * i)] for i in range(replicas // 2)]))
+    held = jnp.concatenate(halves, axis=1)
+    held = jnp.stack([held, swap(held, 1)], axis=1)
+    held = held.reshape(replicas, *value.shape)
+    return jnp.stack(
+        [lax.dynamic_index_in_dim(held, me ^ i, 0, keepdims=False) for i in range(replicas)]
+    )
 
 
 def local(
@@ -525,23 +566,23 @@
     normed2 = (unit2 * gain2).astype(BF16)
     n2_near = line.gather(normed2, (), 1)
     dy_hops = line.gather(cotangent, (None, own_attended[1:]), 2, dy_hops)
-    near_parts = [
-        jnp.concatenate([own, line.near(begun)])
-        for own, begun in ((normed2, n2_near), (cotangent, dy_near))
-    ]
+    near_parts = [line.near(n2_near), line.near(dy_near)]
 
     half = groups // 2
     if half > 2:
         n2, dy = line.gather(normed2, (), 0, n2_near), line.gather(cotangent, (), 0, dy_hops)
         near_parts = [jnp.concatenate(part[:half]) for part in (n2, dy)]
-    near = feed_forward(*near_parts, w_gu, w_down)
+    near = feed_forward(*near_parts, w_gu, w_down, HEAVY)
     if half == 2:
         n2 = line.gather(normed2, (None, None, near[3]), 0, n2_near)
-        dy = line.gather(cotangent, (None, None, n2_near), 0, dy_hops)
+        dy_hops = line.gather(cotangent, (None, None, n2_near), 3, dy_hops)
+        for part, last in zip(dy_hops, after([part[-1] for part in dy_hops], near[3])):
+            part[-1] = last
+        dy = line.gather(cotangent, (), 0, dy_hops)
     n2_parts = [near_parts[0], jnp.concatenate(n2[half:])]
     dy_parts = [near_parts[1], jnp.concatenate(dy[half:])]
     n2_parts[1] = after(n2_parts[1], near[3])
-    far = feed_forward(n2_parts[1], dy_parts[1], w_gu, w_down)
+    far = feed_forward(n2_parts[1], dy_parts[1], w_gu, w_down, LIGHT)
     grad_n2 = line.exchange(cut(near[3])[:half] + cut(far[3])[:half])
 
     def sum_plane(value):
@@ -557,7 +598,7 @@
     gu_grad = gu_grad.reshape(replicas, groups * rows, 2 * ffs)
     gu_grad = sum_plane(gu_grad).reshape(groups, rows, 2 * ffs)
 
-    grad_n2 = after(grad_n2, gu_done)
+    grad_n2 = after(grad_n2, gu_done, cost=HEAVY)
     grad_n2 = sum([part.astype(F32) for part in grad_n2])
     gain2_grad = jnp.sum(grad_n2 * unit2, axis=0)
     grad_h1 = cotangent.astype(F32) + rms_norm_backward(grad_n2, unit2, inv2, gain2)
@@ -568,54 +609,73 @@
         (((1, 2), (0, 2)), ((), ())),
         preferred_element_type=F32,
     ).astype(BF16)
+    heads_there = grad_heads
     grad_heads = line.exchange([grad_heads[:, k * qw : (k + 1) * qw] for k in range(groups)])
-    down = [dot(after(part, grad_attn), w_down, ((1,), (0,))).astype(BF16) for part in hidden]
-    grad_heads = jnp.concatenate(after(grad_heads, down))
+    grad_heads = jnp.concatenate(grad_heads)
+    ga_hops = line.gather(grad_attn, (grad_heads,), 1)
     grad_qkv, own_qkv = attention_backward(
         hl, kvl, q_rot, k_rot, values, attended, lse, grad_heads, cosine, sine, start, place
     )
+    down = [dot(after(part, own_qkv), w_down, ((1,), (0,))).astype(BF16) for part in hidden]
+    down = cut(down[0])[:half] + cut(down[1])[:half]
+    own_qkv = after(own_qkv, [part[1] for part in ga_hops])
     qkv_grad = dot(normed1, grad_qkv, ((0,), (0,))).astype(BF16)
     grad_n1 = dot(own_qkv, w_qkv, ((1,), (1,))).astype(BF16)
-    grad_n1 = line.scatter_sum(cut(grad_n1))
-    n1_hops = line.hops
-    grad_attn_all = line.gather(grad_attn, (grad_heads, own_qkv, n1_hops[0]))
+
+    def by_group(value):
+        return line.exchange([line.at(value, k) for k in range(groups)])
+
+    qkv_grad = qkv_grad.reshape(groups, replicas, rows, qkvw).transpose(1, 2, 0, 3)
+    qkv_grad = qkv_grad.reshape(replicas, rows, groups * qkvw)
+    n1_slots, n1_hops = cut(grad_n1), []
+    for i in range(groups - 1):
+        came = n1_hops[-1] if n1_hops else None
+        gate = [part[-1] for part in ga_hops] if i else ()
+        n1_hops.append(line.scatter_hop(n1_slots, came, groups - 1 - i, gate))
+        if i + 2 < groups:
+            gates = [None] * (i + 1) + [came if i else own_qkv]
+            ga_hops = line.gather(grad_attn, gates, i + 2, ga_hops)
+    gu_grad, down_grad, qkv_grad = after((gu_grad, down_grad, qkv_grad), n1_hops[0])
+    qkv_grad = sum_plane(qkv_grad)
+    down_grad = over_plane(down_grad).reshape(ffs, width)
+    gu_grad = by_group(after(gu_grad, n1_hops[-2]))
+    grad_n1 = sum(part.astype(F32) for part in (n1_slots[0], *n1_hops[-1]))
+    grad_attn_all = line.gather(grad_attn, (), 0, ga_hops)
     inv1 = inverse_rms(x_own)
     unit1 = x_own * inv1
     gain1_grad = jnp.sum(grad_n1 * unit1, axis=0)
     x_grad = (grad_h1 + rms_norm_backward(grad_n1, unit1, inv1, gain1)).astype(BF16)
-    down = after(down, grad_attn_all[-1])
-    down = line.scatter_sum(cut(down[0])[:half] + cut(down[1])[:half])
-    mixed = (h1 + down).astype(BF16)
 
     grad_attn_all = jnp.concatenate(after(grad_attn_all, grad_n1))
     out_grad = dot(attended_low, grad_attn_all, ((0,), (0,))).astype(BF16)
     gain_grads = jnp.stack([gain1_grad, gain2_grad]).reshape(2, groups, replicas, rows)
     gain_grads = gain_grads.transpose(2, 3, 1, 0).astype(BF16)
     gain_grads = jnp.pad(gain_grads, ((0, 0), (0, 0), (0, 0), (0, 128 - 2)))
-    qkv_grad = qkv_grad.reshape(groups, replicas, rows, qkvw).transpose(1, 2, 0, 3)
-    wide = groups * (qkvw + 128)
-    grads = jnp.concatenate([qkv_grad, gain_grads], axis=3).reshape(replicas, rows, wide)
-    grads = jnp.concatenate([grads, out_grad.reshape(replicas, rows, width)], axis=2)
-
-    def by_group(value):
-        return line.exchange([line.at(value, k) for k in range(groups)])
-
-    gu_grad, down_grad = after((gu_grad, down_grad), n1_hops[-2])
-    gu_grad = line.ordered(by_group(gu_grad))
-    down_grad = over_plane(down_grad).reshape(ffs, width)
+    out_grad = out_grad.reshape(replicas, rows, width)
+    gain_grads = gain_grads.reshape(replicas, rows, groups * 128)
+    out_grad = jnp.concatenate([out_grad, gain_grads], axis=2)
+    out_grad = sum_plane(after(out_grad, down_grad, qkv_grad))
+    y_hops = []
+    for hop in range(groups - 1, 0, -1):
+        gate = () if y_hops else n1_hops[-1]
+        y_hops.append(line.scatter_hop(down, y_hops[-1] if y_hops else None, hop, gate))
+    mixed = (h1 + sum(part.astype(F32) for part in (down[0], *y_hops[-1]))).astype(BF16)
+
+    gu_grad = line.ordered(gu_grad)
     gu_grad = jnp.concatenate([part.reshape(rows, 2, ffs) for part in gu_grad], axis=2)
-    gu_grad = over_plane(after(gu_grad, down_grad))
-    grads = sum_plane(after(grads, gu_grad))
-
-    out_grad = grads[:, wide:]
-    grads = jnp.swapaxes(grads[:, :wide].reshape(rows, groups, qkvw + 128), 0, 1)
-    grads = by_group(grads)
+    gu_grad = over_plane(after(gu_grad, out_grad, y_hops[-2]))
+
+    grads = jnp.concatenate(
+        [qkv_grad.reshape(rows, groups, qkvw), out_grad[:, width:].reshape(rows, groups, 128)], axis=2
+    )
+    grads = by_group(jnp.swapaxes(grads, 0, 1))
     gain_grads = sum([part[:, qkvw:].astype(F32) for part in grads]).astype(BF16)
     grads = line.ordered(grads)
     grads = [part[:, :qw] for part in grads] + [
         part[:, qw + j * kw : qw + (j + 1) * kw] for j in range(2) for part in grads
     ]
-    grads = over_plane(after(jnp.concatenate(grads + [out_grad, gain_grads], axis=1), mixed))
+    grads = jnp.concatenate(grads + [out_grad[:, :width], gain_grads], axis=1)
+    grads = gather_plane(grads, replicas, me_r)
     gu_grad = gu_grad.reshape(shard, 2, ff).astype(F32)
     down_grad = down_grad.astype(F32)
     grads = grads.reshape(shard, -1).astype(F32)

time: 1120 us -> 988 us (0.88)
  starting transfers between devices: 234 us -> 137 us
  waiting for transfers between devices: 381 us -> 338 us
    ppermute x27, starting transfers between devices: 154 us -> 59.3 us  [swap(): lax.ppermute(value, 'group', [(i, i ^ slot) for i in range(self.count)])]
    ppermute x27, waiting for transfers between devices: 93.4 us -> 132 us  [swap(): lax.ppermute(value, 'group', [(i, i ^ slot) for i in range(self.count)])]
    ppermute x12, waiting for transfers between devices: 140 us -> 107 us  [gather(): high.append(lax.ppermute(moving[1], 'group', down))]
    all_gather x6 -> x5, waiting for transfers between devices: 30.8 us -> 0.02 us  [over_plane(): return lax.all_gather(value, 'replica', axis=0)]
    ppermute x12 -> x17, waiting for transfers between devices: 94.3 us -> 79.1 us  [the longest x5 33.8 us: swap(): lax.ppermute(part, 'replica', [(i, i ^ bit) for i in range(replicas)])]
    unnamed x204 -> x251, local copies, waits for them, and re-layouts: 49.2 us -> 38.7 us
    slice x27 -> x34, local copies, waits for them, and re-layouts: 21.8 us -> 29.1 us  [mark(): return value[:8, :128]]
    ppermute x12 -> x17, starting transfers between devices: 31 us -> 34.1 us  [the longest x6 19.7 us: scatter_hop(): lax.ppermute(moving[0], 'group', up)]
  transfers between devices with their start and end apart: 72 -> 77, of which waited for: 30 -> 33; matrix products, arithmetic and copies ran while one was open for 23% -> 27% of each run, Pallas kernels for 8% -> 12%
where the time goes in v2:
time: 988 us; the launch traced here: 981 us
  waiting for transfers between devices  338 us (34%)
  Pallas kernels  170 us (17%)
  local copies, waits for them, and re-layouts  140 us (14%)
  starting transfers between devices  137 us (14%)
  other arithmetic  123 us (12%)
  matrix products  56.7 us (6%)
  between operations  16 us (2%)
    ppermute x27, waiting for transfers between devices, swap(): lax.ppermute(value, 'group', [(i, i ^ slot) for i in range(self.count)])  132 us
    ppermute x12, waiting for transfers between devices, gather(): high.append(lax.ppermute(moving[1], 'group', down))  107 us
    pallas_call x2, Pallas kernels, feed_forward(): pl.pallas_call(functools.partial(hidden_kernel, parts), grid=(count // pa...  61.1 us
    ppermute x27, starting transfers between devices, swap(): lax.ppermute(value, 'group', [(i, i ^ slot) for i in range(self.count)])  59.3 us
    pallas_call x2, Pallas kernels, weight_gradient(): pl.pallas_call(functools.partial(product_kernel, parts), grid=(blocks, le...  51 us
    dot_general x7, matrix products, dot(): lax.dot_general(left, right, (dims, ((), ())), preferred_element_type=F32)  46.2 us
    unnamed x251, local copies, waits for them, and re-layouts  38.7 us
    pallas_call x1, Pallas kernels, attention_backward(): pl.pallas_call(functools.partial(backward_kernel, hl, kvl, block), out_sh...  34.6 us
  transfers between devices with their start and end apart: 77, of which 33 were waited for; matrix products, arithmetic and copies ran while one was open for 27% of the time, Pallas kernels for 12%

profile of v2, /device:TPU:0, one launch (start us, length us, event | category | flops | bytes accessed | tf_op | source)
XLA Modules:
  0.0 980.7 jit_solution(12035429161241240117)
XLA Ops:
  24.2 18.4 %collective-permute-done.3.refs_1_ = bf16[64,768]{1,0:T(8,128)(2,1)S(1)} collective-permute-done((bf16[64,768]{1,0:T(8,128)(2,1)S(1)}, bf16[64,768]{1,0:T(8,128)(2,1)S(1)}, u32[]{:S(2)}, u32[]{:S(2)}) %collective-permute-start.3) | collective-permute-done | bytes 98336 | tf_op jit(solution)/shard_map/ppermute | solution.py:359
  97.2 13.2 %collective-permute-done.12 = bf16[256,2048]{1,0:T(8,128)(2,1)} collective-permute-done((bf16[256,2048]{1,0:T(8,128)(2,1)}, bf16[256,2048]{1,0:T(8,128)(2,1)}, u32[]{:S(2)}, u32[]{:S(2)}) %collective-permute-start.12) | collective-permute-done | bytes 1048608 | tf_op jit(solution)/shard_map/ppermute | solution.py:403
  116.9 18.1 %collective-permute-done.14 = bf16[256,2048]{1,0:T(8,128)(2,1)S(1)} collective-permute-done((bf16[256,2048]{1,0:T(8,128)(2,1)}, bf16[256,2048]{1,0:T(8,128)(2,1)S(1)}, u32[]{:S(2)}, u32[]{:S(2)}) %collective-permute-start.14) | collective-permute-done | bytes 1048608 | tf_op jit(solution)/shard_map/ppermute | solution.py:403
  175.8 21.8 %attention_forward.1 = (bf16[1024,512]{1,0:T(8,128)(2,1)}, bf16[1024,128]{1,0:T(8,128)(2,1)}, bf16[1024,128]{1,0:T(8,128)(2,1)}, f32[1024,512]{1,0:T(8,128)}, f3...) custom-call(f32[1024,768]{1,0:T(8,128)} %fusion.89.qkv_ref, f32[1024,128]{1,0:T(8,128)} %copy.171.cos_ref, ...), custom_call_target="tpu_custom_call" | custom-call | flops 1 | bytes 1 | tf_op jit(solution)/shard_map/attention_forward/pallas_call | solution.py:169
  256.3 16.0 %collective-permute-done.20.low_ref = bf16[256,2048]{1,0:T(8,128)(2,1)} collective-permute-done((bf16[256,2048]{1,0:T(8,128)(2,1)S(1)}, bf16[256,2048]{1,0:T(8,128)(2,1)}, u32[]{:S(2)}, u32[]{:S(2)}) %collective-permute-start.20) | collective-permute-done | bytes 1048608 | tf_op jit(solution)/shard_map/ppermute | solution.py:402
  282.6 17.3 %collective-permute-done.31.refs_1_ = bf16[256,2048]{1,0:T(8,128)(2,1)} collective-permute-done((bf16[256,2048]{1,0:T(8,128)(2,1)S(1)}, bf16[256,2048]{1,0:T(8,128)(2,1)}, u32[]{:S(2)}, u32[]{:S(2)}) %collective-permute-start.31) | collective-permute-done | bytes 1048608 | tf_op jit(solution)/shard_map/ppermute | solution.py:403
  311.5 30.5 %feed_forward.2 = (bf16[512,2048]{1,0:T(8,128)(2,1)}, bf16[512,2048]{1,0:T(8,128)(2,1)}, bf16[512,2048]{1,0:T(8,128)(2,1)}, bf16[512,2048]{1,0:T(8,128)(2,1)}) custom-call(bf16[512,2048]{1,0:T(8,128)(2,1)} %copy-done.2, bf16[512,2048]{1,0:T(8,128)(2,1)} %copy-done.10, bf16[8,2048,512]{2,1,0:T(8,128)(2,1)} %bitcast.178, bf16[2048,2048]{1,0:T(8,128)(2,1)} %down_ref.3), custom_call_target="tpu_custom_call" | custom-call | flops 299999985664 | bytes 1 | tf_op jit(solution)/shard_map/feed_forward/pallas_call | solution.py:245
  355.1 18.6 %collective-permute-done.29 = bf16[256,2048]{1,0:T(8,128)(2,1)} collective-permute-done((bf16[256,2048]{1,0:T(8,128)(2,1)}, bf16[256,2048]{1,0:T(8,128)(2,1)}, u32[]{:S(2)}, u32[]{:S(2)}) %collective-permute-start.29) | collective-permute-done | bytes 1048608 | tf_op jit(solution)/shard_map/ppermute | solution.py:403
  378.2 30.6 %feed_forward.3 = (bf16[512,2048]{1,0:T(8,128)(2,1)}, bf16[512,2048]{1,0:T(8,128)(2,1)}, bf16[512,2048]{1,0:T(8,128)(2,1)}, bf16[512,2048]{1,0:T(8,128)(2,1)}) custom-call(bf16[512,2048]{1,0:T(8,128)(2,1)} %after.32.n2_ref.refs_1_, bf16[512,2048]{1,0:T(8,128)(2,1)} %pad_maximum_fusion.5.dy_ref.refs_3_, bf16[8,2048,512]{2,1,0:T(8,128)(2,1)} %bitcast.179, ...), custom_call_target="tpu_custom_call" | custom-call | flops 1 | bytes 1 | tf_op jit(solution)/shard_map/feed_forward/pallas_call | solution.py:245
  408.8 17.6 %weight_gradient.2 = (bf16[2048,2048]{1,0:T(8,128)(2,1)}, f32[8,128]{1,0:T(8,128)}) custom-call(bf16[512,2048]{1,0:T(8,128)(2,1)} %get-tuple-element.85.refs_0_, bf16[512,2048]{1,0:T(8,128)(2,1)} %get-tuple-element.101.refs_1_.refs_0_, bf16[512,2048]{1,0:T(8,128)(2,1)} %copy-done.10, bf16[512,2048]{1,0:T(8,128)(2,1)} %pad_maximum_fusion.5.dy_ref.refs_3_), custom_call_target="tpu_custom_call" | custom-call | flops 1 | bytes 1 | tf_op jit(solution)/shard_map/weight_gradient/pallas_call | solution.py:304
  435.4 33.4 %weight_gradient.3 = (bf16[8,4,64,4096]{3,2,1,0:T(8,128)(2,1)}, f32[8,128]{1,0:T(8,128)}) custom-call(bf16[512,2048]{1,0:T(8,128)(2,1)} %after.36.refs_0_, bf16[512,2048]{1,0:T(8,128)(2,1)} %after.32.n2_ref.refs_1_, bf16[512,2048]{1,0:T(8,128)(2,1)} %get-tuple-element.103.refs_2_, bf16[512,2048]{1,0:T(8,128)(2,1)} %get-tuple-element.104.refs_3_, ...), custom_call_target="tpu_custom_call" | custom-call | flops 1 | bytes 1 | tf_op jit(solution)/shard_map/weight_gradient/pallas_call | solution.py:304
  469.4 34.7 %collective-permute-done.34.refs_2_ = bf16[256,2048]{1,0:T(8,128)(2,1)S(1)} collective-permute-done((bf16[256,2048]{1,0:T(8,128)(2,1)}, bf16[256,2048]{1,0:T(8,128)(2,1)S(1)}, u32[]{:S(2)}, u32[]{:S(2)}) %collective-permute-start.34) | collective-permute-done | bytes 1048608 | tf_op jit(solution)/shard_map/ppermute | solution.py:359
  521.4 17.7 %collective-permute-start.37 = (bf16[256,512]{1,0:T(8,128)(2,1)}, bf16[256,512]{1,0:T(8,128)(2,1)}, u32[]{:S(2)}, u32[]{:S(2)}) collective-permute-start(bf16[256,512]{1,0:T(8,128)(2,1)} %get-tuple-element.194), channel_id=1, source_target_pairs={{0,2},{1,3},{2,0},{3,1},{4,6},{5,7},{6,4},{7,5},{8,10},{9,11},{10,... | collective-permute-start | bytes 786440 | tf_op jit(solution)/shard_map/ppermute | solution.py:359
  557.3 34.6 %attention_backward.1 = (bf16[1024,768]{1,0:T(8,128)(2,1)}, bf16[1024,768]{1,0:T(8,128)(2,1)}) custom-call(bf16[1024,512]{1,0:T(8,128)(2,1)} %get-tuple-element.86.q_ref, bf16[1024,128]{1,0:T(8,128)(2,1)} %get-tuple-element.87.k_ref, bf16[1024,128]{1,0:T(8,128)(2,1)} %get-tuple-element.88.v_ref, f32[1024,512]{1,0:T(8,128)} %get-tuple-element.89.att_ref, ...), custom_call_target="tpu_custom_call" | custom-call | flops 40000000000 | bytes 1 | tf_op jit(solution)/shard_map/attention_backward/pallas_call | solution.py:187
  643.8 13.9 %collective-permute-done.44.refs_1_ = bf16[256,2048]{1,0:T(8,128)(2,1)S(1)} collective-permute-done((bf16[256,2048]{1,0:T(8,128)(2,1)}, bf16[256,2048]{1,0:T(8,128)(2,1)S(1)}, u32[]{:S(2)}, u32[]{:S(2)}) %collective-permute-start.44) | collective-permute-done | bytes 1048608 | tf_op jit(solution)/shard_map/ppermute | solution.py:403
  702.9 10.4 %collective-permute-done.49 = bf16[256,2048]{1,0:T(8,128)(2,1)S(1)} collective-permute-done((bf16[256,2048]{1,0:T(8,128)(2,1)}, bf16[256,2048]{1,0:T(8,128)(2,1)S(1)}, u32[]{:S(2)}, u32[]{:S(2)}) %collective-permute-start.49) | collective-permute-done | bytes 1048608 | tf_op jit(solution)/shard_map/ppermute | solution.py:426
  762.4 12.7 %collective-permute-done.52 = bf16[256,2048]{1,0:T(8,128)(2,1)} collective-permute-done((bf16[256,2048]{1,0:T(8,128)(2,1)}, bf16[256,2048]{1,0:T(8,128)(2,1)}, u32[]{:S(2)}, u32[]{:S(2)}) %collective-permute-start.52) | collective-permute-done | bytes 1048608 | tf_op jit(solution)/shard_map/ppermute | solution.py:426
  777.6 12.6 %collective-permute-done.65 = bf16[64,4096]{1,0:T(8,128)(2,1)S(1)} collective-permute-done((bf16[64,4096]{1,0:T(8,128)(2,1)S(1)}, bf16[64,4096]{1,0:T(8,128)(2,1)S(1)}, u32[]{:S(2)}, u32[]{:S(2)}) %collective-permute-start.65) | collective-permute-done | bytes 524320 | tf_op jit(solution)/shard_map/ppermute | solution.py:359
  790.2 25.4 %collective-permute-done.66 = bf16[64,4096]{1,0:T(8,128)(2,1)S(1)} collective-permute-done((bf16[64,4096]{1,0:T(8,128)(2,1)S(1)}, bf16[64,4096]{1,0:T(8,128)(2,1)S(1)}, u32[]{:S(2)}, u32[]{:S(2)}) %collective-permute-start.66) | collective-permute-done | bytes 524320 | tf_op jit(solution)/shard_map/ppermute | solution.py:359
  847.2 15.1 %collective-permute-done.62 = bf16[1,32,5248]{2,1,0:T(8,128)(2,1)S(1)} collective-permute-done((bf16[1,32,5248]{2,1,0:T(8,128)(2,1)S(1)}, bf16[1,32,5248]{2,1,0:T(8,128)(2,1)S(1)}, u32[]{:S(2)}, u32[]{:S(2)}) %collective-permute-start.62) | collective-permute-done | bytes 335904 | tf_op jit(solution)/shard_map/ppermute | solution.py:448
  865.4 18.3 %collective-permute-done.63 = bf16[2,32,5248]{2,1,0:T(8,128)(2,1)S(1)} collective-permute-done((bf16[2,32,5248]{2,1,0:T(8,128)(2,1)S(1)}, bf16[2,32,5248]{2,1,0:T(8,128)(2,1)S(1)}, u32[]{:S(2)}, u32[]{:S(2)}) %collective-permute-start.63) | collective-permute-done | bytes 671776 | tf_op jit(solution)/shard_map/ppermute | solution.py:448
  902.7 14.6 %collective-permute-done.56 = bf16[256,2048]{1,0:T(8,128)(2,1)} collective-permute-done((bf16[256,2048]{1,0:T(8,128)(2,1)}, bf16[256,2048]{1,0:T(8,128)(2,1)}, u32[]{:S(2)}, u32[]{:S(2)}) %collective-permute-start.56) | collective-permute-done | bytes 1048608 | tf_op jit(solution)/shard_map/ppermute | solution.py:426
  921.7 12.1 %convert_element_type.187 = f32[2048,2048]{1,0:T(8,128)} convert(bf16[2048,2048]{1,0:T(8,128)(2,1)} %all-gather.17.cloned.1.call-done) | non-fusion elementwise | flops 4194304 | bytes 25165824 | tf_op jit(solution)/shard_map/convert_element_type | solution.py:680
  956.1 17.7 %convert_element_type.190 = f32[512,2,8192]{2,1,0:T(2,128)} convert(bf16[512,2,8192]{2,1,0:T(2,128)(2,1)} %all-gather.19.cloned.1.call-done) | non-fusion elementwise | flops 8388608 | bytes 50331648 | tf_op jit(solution)/shard_map/convert_element_type | solution.py:679
  (585 shorter events, 489.6 us)
Async XLA Ops:
  7.2 155.5 %all-gather.11.cloned.1.call-start = ((), (), s32[]{:S(2)}) async-start(), calls=%async_computation.8 | async-start | bytes 3538944 | tf_op jit(solution)/shard_map/all_gather | solution.py:498
  7.2 59.2 %collective-permute-start.9 = (bf16[256,2048]{1,0:T(8,128)(2,1)}, bf16[256,2048]{1,0:T(8,128)(2,1)S(1)}, u32[]{:S(2)}, u32[]{:S(2)}) collective-permute-start(bf16[256,2048]{1,0:T(8,128)(2,1)} %param.11), channel_id=1, source_target_pairs={{0,1},{1,2},{2,3},{4,5},{5,6},{6,7},{8,9},{9,10},{10,11},{12,13},{... | collective-permute-start | bytes 3145736 | tf_op jit(solution)/shard_map/ppermute | solution.py:402
  12.4 54.0 %collective-permute-start.10 = (bf16[256,2048]{1,0:T(8,128)(2,1)}, bf16[256,2048]{1,0:T(8,128)(2,1)}, u32[]{:S(2)}, u32[]{:S(2)}) collective-permute-start(bf16[256,2048]{1,0:T(8,128)(2,1)} %param.11), channel_id=1, source_target_pairs={{1,0},{2,1},{3,2},{5,4},{6,5},{7,6},{9,8},{10,9},{11,10},{13,12},{... | collective-permute-start | bytes 3145736 | tf_op jit(solution)/shard_map/ppermute | solution.py:403
  69.6 161.6 %all-gather.13.cloned.1.call-start = ((), (), s32[]{:S(2)}) async-start(), calls=%async_computation.9 | async-start | bytes 9437184 | tf_op jit(solution)/shard_map/all_gather | solution.py:498
  71.7 239.8 %all-gather.15.cloned.1.call-start = ((), (), s32[]{:S(2)}) async-start(), calls=%async_computation.10 | async-start | bytes 18874368 | tf_op jit(solution)/shard_map/all_gather | solution.py:498
  142.8 55.9 %collective-permute-start.22 = (bf16[512,512]{1,0:T(8,128)(2,1)}, bf16[512,512]{1,0:T(8,128)(2,1)}, u32[]{:S(2)}, u32[]{:S(2)}) collective-permute-start(bf16[512,512]{1,0:T(8,128)(2,1)} %get-tuple-element.189), channel_id=1, source_target_pairs={{0,1},{1,0},{2,3},{3,2},{4,5},{5,4},{6,7},{7,6},{8,9},{9,8},{10,11... | collective-permute-start | bytes 1572872 | tf_op jit(solution)/shard_map/ppermute | solution.py:359
  145.4 54.2 %collective-permute-start.23 = (bf16[512,512]{1,0:T(8,128)(2,1)}, bf16[512,512]{1,0:T(8,128)(2,1)}, u32[]{:S(2)}, u32[]{:S(2)}) collective-permute-start(bf16[512,512]{1,0:T(8,128)(2,1)} %get-tuple-element.188), channel_id=1, source_target_pairs={{0,2},{1,3},{2,0},{3,1},{4,6},{5,7},{6,4},{7,5},{8,10},{9,11},{10,... | collective-permute-start | bytes 1572872 | tf_op jit(solution)/shard_map/ppermute | solution.py:359
  146.8 52.8 %collective-permute-start.24 = (bf16[512,512]{1,0:T(8,128)(2,1)}, bf16[512,512]{1,0:T(8,128)(2,1)}, u32[]{:S(2)}, u32[]{:S(2)}) collective-permute-start(bf16[512,512]{1,0:T(8,128)(2,1)} %get-tuple-element.187), channel_id=1, source_target_pairs={{0,3},{1,2},{2,1},{3,0},{4,7},{5,6},{6,5},{7,4},{8,11},{9,10},{10,... | collective-permute-start | bytes 1572872 | tf_op jit(solution)/shard_map/ppermute | solution.py:359
  202.9 425.1 %reduce-scatter.7.cloned.1.call-start = ((), (), s32[]{:S(2)}) async-start(), calls=%async_computation.5 | async-start | bytes 9437184 | tf_op jit(solution)/shard_map/reduce_scatter | solution.py:589
  254.4 45.5 %collective-permute-start.31 = (bf16[256,2048]{1,0:T(8,128)(2,1)S(1)}, bf16[256,2048]{1,0:T(8,128)(2,1)}, u32[]{:S(2)}, u32[]{:S(2)}) collective-permute-start(bf16[256,2048]{1,0:T(8,128)(2,1)S(1)} %copy-done.7), channel_id=1, source_target_pairs={{1,0},{2,1},{5,4},{6,5},{9,8},{10,9},{13,12},{14,13},{17,16},{18,1... | collective-permute-start | bytes 3145736 | tf_op jit(solution)/shard_map/ppermute | solution.py:403
  299.9 51.6 %collective-permute-start.32 = (bf16[256,2048]{1,0:T(8,128)(2,1)}, bf16[256,2048]{1,0:T(8,128)(2,1)}, u32[]{:S(2)}, u32[]{:S(2)}) collective-permute-start(bf16[256,2048]{1,0:T(8,128)(2,1)} %get-tuple-element.96), channel_id=1, source_target_pairs={{2,3},{6,7},{10,11},{14,15},{18,19},{22,23},{26,27},{30,31}} | collective-permute-start | bytes 3145736 | tf_op jit(solution)/shard_map/ppermute | solution.py:402
  301.6 49.9 %collective-permute-start.33 = (bf16[256,2048]{1,0:T(8,128)(2,1)}, bf16[256,2048]{1,0:T(8,128)(2,1)}, u32[]{:S(2)}, u32[]{:S(2)}) collective-permute-start(bf16[256,2048]{1,0:T(8,128)(2,1)} %get-tuple-element.97), channel_id=1, source_target_pairs={{1,0},{5,4},{9,8},{13,12},{17,16},{21,20},{25,24},{29,28}} | collective-permute-start | bytes 3145736 | tf_op jit(solution)/shard_map/ppermute | solution.py:403
  426.4 201.6 %reduce-scatter.5.cloned.1.call-start = ((), (), s32[]{:S(2)}) async-start(), calls=%async_computation.4 | async-start | bytes 18874368 | tf_op jit(solution)/shard_map/reduce_scatter | solution.py:589
  431.9 72.1 %collective-permute-start.34 = (bf16[256,2048]{1,0:T(8,128)(2,1)}, bf16[256,2048]{1,0:T(8,128)(2,1)S(1)}, u32[]{:S(2)}, u32[]{:S(2)}) collective-permute-start(bf16[256,2048]{1,0:T(8,128)(2,1)} %get-tuple-element.180), channel_id=1, source_target_pairs={{0,2},{1,3},{2,0},{3,1},{4,6},{5,7},{6,4},{7,5},{8,10},{9,11},{10,... | collective-permute-start | bytes 3145736 | tf_op jit(solution)/shard_map/ppermute | solution.py:359
  431.9 72.2 %collective-permute-start.35 = (bf16[256,2048]{1,0:T(8,128)(2,1)}, bf16[256,2048]{1,0:T(8,128)(2,1)}, u32[]{:S(2)}, u32[]{:S(2)}) collective-permute-start(bf16[256,2048]{1,0:T(8,128)(2,1)} %get-tuple-element.179), channel_id=1, source_target_pairs={{0,3},{1,2},{2,1},{3,0},{4,7},{5,6},{6,5},{7,4},{8,11},{9,10},{10,... | collective-permute-start | bytes 3145736 | tf_op jit(solution)/shard_map/ppermute | solution.py:359
  468.9 274.7 %reduce-scatter.9.cloned.1.call-start = ((), (), s32[]{:S(2)}) async-start(), calls=%async_computation.6 | async-start | bytes 3538944 | tf_op jit(solution)/shard_map/reduce_scatter | solution.py:589
  540.7 52.4 %collective-permute-start.39 = (bf16[256,2048]{1,0:T(8,128)(2,1)}, bf16[256,2048]{1,0:T(8,128)(2,1)S(1)}, u32[]{:S(2)}, u32[]{:S(2)}) collective-permute-start(bf16[256,2048]{1,0:T(8,128)(2,1)} %after.40), channel_id=1, source_target_pairs={{0,1},{1,2},{2,3},{4,5},{5,6},{6,7},{8,9},{9,10},{10,11},{12,13},{... | collective-permute-start | bytes 3145736 | tf_op jit(solution)/shard_map/ppermute | solution.py:402
  544.7 49.0 %collective-permute-start.40 = (bf16[256,2048]{1,0:T(8,128)(2,1)}, bf16[256,2048]{1,0:T(8,128)(2,1)S(1)}, u32[]{:S(2)}, u32[]{:S(2)}) collective-permute-start(bf16[256,2048]{1,0:T(8,128)(2,1)} %after.40), channel_id=1, source_target_pairs={{1,0},{2,1},{3,2},{5,4},{6,5},{7,6},{9,8},{10,9},{11,10},{13,12},{... | collective-permute-start | bytes 3145736 | tf_op jit(solution)/shard_map/ppermute | solution.py:403
  628.0 116.8 %all-gather.17.cloned.1.call-start = ((), (), s32[]{:S(2)}) async-start(), calls=%async_computation.11 | async-start | bytes 9437184 | tf_op jit(solution)/shard_map/all_gather | solution.py:498
  628.8 203.2 %reduce-scatter.11.cloned.1.call-start = ((), (), s32[]{:S(2)}) async-start(), calls=%async_computation.7 | async-start | bytes 2949120 | tf_op jit(solution)/shard_map/reduce_scatter | solution.py:589
  746.2 210.0 %all-gather.19.cloned.1.call-start = ((), (), s32[]{:S(2)}) async-start(), calls=%async_computation.12 | async-start | bytes 18874368 | tf_op jit(solution)/shard_map/all_gather | solution.py:498
  759.8 55.8 %collective-permute-start.66 = (bf16[64,4096]{1,0:T(8,128)(2,1)S(1)}, bf16[64,4096]{1,0:T(8,128)(2,1)S(1)}, u32[]{:S(2)}, u32[]{:S(2)}) collective-permute-start(bf16[64,4096]{1,0:T(8,128)(2,1)S(1)} %get-tuple-element.175), channel_id=1, source_target_pairs={{0,2},{1,3},{2,0},{3,1},{4,6},{5,7},{6,4},{7,5},{8,10},{9,11},{10,... | collective-permute-start | bytes 1572872 | tf_op jit(solution)/shard_map/ppermute | solution.py:359
  759.8 55.8 %collective-permute-start.67 = (bf16[64,4096]{1,0:T(8,128)(2,1)S(1)}, bf16[64,4096]{1,0:T(8,128)(2,1)S(1)}, u32[]{:S(2)}, u32[]{:S(2)}) collective-permute-start(bf16[64,4096]{1,0:T(8,128)(2,1)S(1)} %get-tuple-element.174), channel_id=1, source_target_pairs={{0,1},{1,0},{2,3},{3,2},{4,5},{5,4},{6,7},{7,6},{8,9},{9,8},{10,11... | collective-permute-start | bytes 1572872 | tf_op jit(solution)/shard_map/ppermute | solution.py:359
  885.9 48.3 %collective-permute-start.64 = (bf16[4,64,5248]{2,1,0:T(8,128)(2,1)}, bf16[4,64,5248]{2,1,0:T(8,128)(2,1)}, u32[]{:S(2)}, u32[]{:S(2)}) collective-permute-start(bf16[4,64,5248]{2,1,0:T(8,128)(2,1)} %maximum_maximum_fusion), channel_id=1, source_target_pairs={{0,4},{4,0},{8,12},{12,8},{16,20},{20,16},{24,28},{28,24},{1,5},{5... | collective-permute-start | bytes 8060936 | tf_op jit(solution)/shard_map/ppermute | solution.py:448
  (163 other events, 2421.9 us)
Sparse Core Ops, SparseCore 0:
  69.7 35.0 all-gather.10
  107.2 54.3 all-gather.12
  203.0 94.8 all-gather.14
  426.5 69.5 reduce-scatter.6
  500.5 115.9 reduce-scatter.4
  628.1 47.3 reduce-scatter.8
  677.4 54.3 all-gather.16
  746.3 43.1 reduce-scatter.10
  833.3 103.3 all-gather.18

commit v3 on v2

--- a/solution.py
+++ b/solution.py
@@ -657,13 +657,13 @@
     out_grad = sum_plane(after(out_grad, down_grad, qkv_grad))
     y_hops = []
     for hop in range(groups - 1, 0, -1):
-        gate = () if y_hops else n1_hops[-1]
+        gate = (n1_hops[-1], gu_grad[1:], ())[min(len(y_hops), 2)]
         y_hops.append(line.scatter_hop(down, y_hops[-1] if y_hops else None, hop, gate))
     mixed = (h1 + sum(part.astype(F32) for part in (down[0], *y_hops[-1]))).astype(BF16)
 
     gu_grad = line.ordered(gu_grad)
     gu_grad = jnp.concatenate([part.reshape(rows, 2, ffs) for part in gu_grad], axis=2)
-    gu_grad = over_plane(after(gu_grad, out_grad, y_hops[-2]))
+    gu_grad = over_plane(after(gu_grad, out_grad, y_hops[0]))
 
     grads = jnp.concatenate(
         [qkv_grad.reshape(rows, groups, qkvw), out_grad[:, width:].reshape(rows, groups, 128)], axis=2

time: 988 us -> 1000 us (1.012)
  starting transfers between devices: 137 us -> 151 us
    ppermute x12, starting transfers between devices: 16.7 us -> 27.6 us  [gather(): high.append(lax.ppermute(moving[1], 'group', down))]
    slice x34 -> x37, local copies, waits for them, and re-layouts: 29.1 us -> 35.6 us  [mark(): return value[:8, :128]]
    unnamed x251 -> x243, local copies, waits for them, and re-layouts: 38.7 us -> 34.9 us
  transfers between devices with their start and end apart: 77 -> 77, of which waited for: 33 -> 33; matrix products, arithmetic and copies ran while one was open for 27% -> 26% of each run, Pallas kernels for 12% -> 12%
where the time goes in v3:
time: 1000 us; the launch traced here: 991 us
  waiting for transfers between devices  333 us (33%)
  Pallas kernels  170 us (17%)
  starting transfers between devices  151 us (15%)
  local copies, waits for them, and re-layouts  143 us (14%)
  other arithmetic  123 us (12%)
  matrix products  55 us (6%)
  between operations  15.9 us (2%)
    ppermute x27, waiting for transfers between devices, swap(): lax.ppermute(value, 'group', [(i, i ^ slot) for i in range(self.count)])  123 us
    ppermute x12, waiting for transfers between devices, gather(): high.append(lax.ppermute(moving[1], 'group', down))  109 us
    pallas_call x2, Pallas kernels, feed_forward(): pl.pallas_call(functools.partial(hidden_kernel, parts), grid=(count // pa...  61.1 us
    ppermute x27, starting transfers between devices, swap(): lax.ppermute(value, 'group', [(i, i ^ slot) for i in range(self.count)])  55.8 us
    pallas_call x2, Pallas kernels, weight_gradient(): pl.pallas_call(functools.partial(product_kernel, parts), grid=(blocks, le...  51.1 us
    dot_general x7, matrix products, dot(): lax.dot_general(left, right, (dims, ((), ())), preferred_element_type=F32)  44.5 us
    slice x37, local copies, waits for them, and re-layouts, mark(): return value[:8, :128]  35.6 us
    unnamed x243, local copies, waits for them, and re-layouts  34.9 us
  transfers between devices with their start and end apart: 77, of which 33 were waited for; matrix products, arithmetic and copies ran while one was open for 26% of the time, Pallas kernels for 12%

profile of v3, /device:TPU:0, one launch (start us, length us, event | category | flops | bytes accessed | tf_op | source)
XLA Modules:
  0.0 990.8 jit_solution(15364339388367707278)
XLA Ops:
  24.2 18.4 %collective-permute-done.3.refs_1_ = bf16[64,768]{1,0:T(8,128)(2,1)S(1)} collective-permute-done((bf16[64,768]{1,0:T(8,128)(2,1)S(1)}, bf16[64,768]{1,0:T(8,128)(2,1)S(1)}, u32[]{:S(2)}, u32[]{:S(2)}) %collective-permute-start.3) | collective-permute-done | bytes 98336 | tf_op jit(solution)/shard_map/ppermute | solution.py:359
  97.2 13.2 %collective-permute-done.12 = bf16[256,2048]{1,0:T(8,128)(2,1)} collective-permute-done((bf16[256,2048]{1,0:T(8,128)(2,1)}, bf16[256,2048]{1,0:T(8,128)(2,1)}, u32[]{:S(2)}, u32[]{:S(2)}) %collective-permute-start.12) | collective-permute-done | bytes 1048608 | tf_op jit(solution)/shard_map/ppermute | solution.py:403
  116.9 18.1 %collective-permute-done.14 = bf16[256,2048]{1,0:T(8,128)(2,1)S(1)} collective-permute-done((bf16[256,2048]{1,0:T(8,128)(2,1)}, bf16[256,2048]{1,0:T(8,128)(2,1)S(1)}, u32[]{:S(2)}, u32[]{:S(2)}) %collective-permute-start.14) | collective-permute-done | bytes 1048608 | tf_op jit(solution)/shard_map/ppermute | solution.py:403
  138.2 13.2 %collective-permute-start.16 = (bf16[256,2048]{1,0:T(8,128)(2,1)}, bf16[256,2048]{1,0:T(8,128)(2,1)S(1)}, u32[]{:S(2)}, u32[]{:S(2)}) collective-permute-start(bf16[256,2048]{1,0:T(8,128)(2,1)} %after.28), channel_id=1, source_target_pairs={{1,0},{2,1},{3,2},{5,4},{6,5},{7,6},{9,8},{10,9},{11,10},{13,12},{... | collective-permute-start | bytes 3145736 | tf_op jit(solution)/shard_map/ppermute | solution.py:403
  179.7 21.8 %attention_forward.1 = (bf16[1024,512]{1,0:T(8,128)(2,1)}, bf16[1024,128]{1,0:T(8,128)(2,1)}, bf16[1024,128]{1,0:T(8,128)(2,1)}, f32[1024,512]{1,0:T(8,128)}, f3...) custom-call(f32[1024,768]{1,0:T(8,128)} %fusion.89.qkv_ref, f32[1024,128]{1,0:T(8,128)} %copy.173.cos_ref, ...), custom_call_target="tpu_custom_call" | custom-call | flops 1 | bytes 1 | tf_op jit(solution)/shard_map/attention_forward/pallas_call | solution.py:169
  256.3 15.5 %collective-permute-done.20.low_ref = bf16[256,2048]{1,0:T(8,128)(2,1)} collective-permute-done((bf16[256,2048]{1,0:T(8,128)(2,1)S(1)}, bf16[256,2048]{1,0:T(8,128)(2,1)}, u32[]{:S(2)}, u32[]{:S(2)}) %collective-permute-start.20) | collective-permute-done | bytes 1048608 | tf_op jit(solution)/shard_map/ppermute | solution.py:402
  282.7 16.8 %collective-permute-done.31.refs_1_ = bf16[256,2048]{1,0:T(8,128)(2,1)} collective-permute-done((bf16[256,2048]{1,0:T(8,128)(2,1)S(1)}, bf16[256,2048]{1,0:T(8,128)(2,1)}, u32[]{:S(2)}, u32[]{:S(2)}) %collective-permute-start.31) | collective-permute-done | bytes 1048608 | tf_op jit(solution)/shard_map/ppermute | solution.py:403
  311.0 30.5 %feed_forward.2 = (bf16[512,2048]{1,0:T(8,128)(2,1)}, bf16[512,2048]{1,0:T(8,128)(2,1)}, bf16[512,2048]{1,0:T(8,128)(2,1)}, bf16[512,2048]{1,0:T(8,128)(2,1)}) custom-call(bf16[512,2048]{1,0:T(8,128)(2,1)} %copy-done.2, bf16[512,2048]{1,0:T(8,128)(2,1)} %copy-done.10, bf16[8,2048,512]{2,1,0:T(8,128)(2,1)} %bitcast.178, bf16[2048,2048]{1,0:T(8,128)(2,1)} %down_ref.3), custom_call_target="tpu_custom_call" | custom-call | flops 299999985664 | bytes 1 | tf_op jit(solution)/shard_map/feed_forward/pallas_call | solution.py:245
  354.2 18.0 %collective-permute-done.29 = bf16[256,2048]{1,0:T(8,128)(2,1)} collective-permute-done((bf16[256,2048]{1,0:T(8,128)(2,1)}, bf16[256,2048]{1,0:T(8,128)(2,1)}, u32[]{:S(2)}, u32[]{:S(2)}) %collective-permute-start.29) | collective-permute-done | bytes 1048608 | tf_op jit(solution)/shard_map/ppermute | solution.py:403
  376.8 30.6 %feed_forward.3 = (bf16[512,2048]{1,0:T(8,128)(2,1)}, bf16[512,2048]{1,0:T(8,128)(2,1)}, bf16[512,2048]{1,0:T(8,128)(2,1)}, bf16[512,2048]{1,0:T(8,128)(2,1)}) custom-call(bf16[512,2048]{1,0:T(8,128)(2,1)} %after.33.n2_ref.refs_1_, bf16[512,2048]{1,0:T(8,128)(2,1)} %pad_maximum_fusion.5.dy_ref.refs_3_, bf16[8,2048,512]{2,1,0:T(8,128)(2,1)} %bitcast.179, ...), custom_call_target="tpu_custom_call" | custom-call | flops 1 | bytes 1 | tf_op jit(solution)/shard_map/feed_forward/pallas_call | solution.py:245
  407.4 17.6 %weight_gradient.2 = (bf16[2048,2048]{1,0:T(8,128)(2,1)}, f32[8,128]{1,0:T(8,128)}) custom-call(bf16[512,2048]{1,0:T(8,128)(2,1)} %get-tuple-element.87.refs_0_, bf16[512,2048]{1,0:T(8,128)(2,1)} %get-tuple-element.103.refs_1_.refs_0_, bf16[512,2048]{1,0:T(8,128)(2,1)} %copy-done.10, bf16[512,2048]{1,0:T(8,128)(2,1)} %pad_maximum_fusion.5.dy_ref.refs_3_), custom_call_target="tpu_custom_call" | custom-call | flops 1 | bytes 1 | tf_op jit(solution)/shard_map/weight_gradient/pallas_call | solution.py:304
  434.1 33.5 %weight_gradient.3 = (bf16[8,4,64,4096]{3,2,1,0:T(8,128)(2,1)}, f32[8,128]{1,0:T(8,128)}) custom-call(bf16[512,2048]{1,0:T(8,128)(2,1)} %after.37.refs_0_, bf16[512,2048]{1,0:T(8,128)(2,1)} %after.33.n2_ref.refs_1_, bf16[512,2048]{1,0:T(8,128)(2,1)} %get-tuple-element.105.refs_2_, bf16[512,2048]{1,0:T(8,128)(2,1)} %get-tuple-element.106.refs_3_, ...), custom_call_target="tpu_custom_call" | custom-call | flops 1 | bytes 1 | tf_op jit(solution)/shard_map/weight_gradient/pallas_call | solution.py:304
  468.0 34.6 %collective-permute-done.34.refs_2_ = bf16[256,2048]{1,0:T(8,128)(2,1)S(1)} collective-permute-done((bf16[256,2048]{1,0:T(8,128)(2,1)}, bf16[256,2048]{1,0:T(8,128)(2,1)S(1)}, u32[]{:S(2)}, u32[]{:S(2)}) %collective-permute-start.34) | collective-permute-done | bytes 1048608 | tf_op jit(solution)/shard_map/ppermute | solution.py:359
  519.9 17.4 %collective-permute-start.37 = (bf16[256,512]{1,0:T(8,128)(2,1)}, bf16[256,512]{1,0:T(8,128)(2,1)}, u32[]{:S(2)}, u32[]{:S(2)}) collective-permute-start(bf16[256,512]{1,0:T(8,128)(2,1)} %get-tuple-element.198), channel_id=1, source_target_pairs={{0,2},{1,3},{2,0},{3,1},{4,6},{5,7},{6,4},{7,5},{8,10},{9,11},{10,... | collective-permute-start | bytes 786440 | tf_op jit(solution)/shard_map/ppermute | solution.py:359
  555.5 34.6 %attention_backward.1 = (bf16[1024,768]{1,0:T(8,128)(2,1)}, bf16[1024,768]{1,0:T(8,128)(2,1)}) custom-call(bf16[1024,512]{1,0:T(8,128)(2,1)} %get-tuple-element.88.q_ref, bf16[1024,128]{1,0:T(8,128)(2,1)} %get-tuple-element.89.k_ref, bf16[1024,128]{1,0:T(8,128)(2,1)} %get-tuple-element.90.v_ref, f32[1024,512]{1,0:T(8,128)} %get-tuple-element.91.att_ref, ...), custom_call_target="tpu_custom_call" | custom-call | flops 40000000000 | bytes 1 | tf_op jit(solution)/shard_map/attention_backward/pallas_call | solution.py:187
  630.1 22.9 %collective-permute-done.44.refs_1_ = bf16[256,2048]{1,0:T(8,128)(2,1)S(1)} collective-permute-done((bf16[256,2048]{1,0:T(8,128)(2,1)}, bf16[256,2048]{1,0:T(8,128)(2,1)S(1)}, u32[]{:S(2)}, u32[]{:S(2)}) %collective-permute-start.44) | collective-permute-done | bytes 1048608 | tf_op jit(solution)/shard_map/ppermute | solution.py:403
  771.9 12.7 %collective-permute-done.51 = bf16[256,2048]{1,0:T(8,128)(2,1)} collective-permute-done((bf16[256,2048]{1,0:T(8,128)(2,1)}, bf16[256,2048]{1,0:T(8,128)(2,1)}, u32[]{:S(2)}, u32[]{:S(2)}) %collective-permute-start.51) | collective-permute-done | bytes 1048608 | tf_op jit(solution)/shard_map/ppermute | solution.py:426
  795.7 11.0 %collective-permute-done.54 = bf16[64,4096]{1,0:T(8,128)(2,1)S(1)} collective-permute-done((bf16[64,4096]{1,0:T(8,128)(2,1)S(1)}, bf16[64,4096]{1,0:T(8,128)(2,1)S(1)}, u32[]{:S(2)}, u32[]{:S(2)}) %collective-permute-start.54) | collective-permute-done | bytes 524320 | tf_op jit(solution)/shard_map/ppermute | solution.py:359
  806.7 10.1 %collective-permute-done.55 = bf16[64,4096]{1,0:T(8,128)(2,1)S(1)} collective-permute-done((bf16[64,4096]{1,0:T(8,128)(2,1)S(1)}, bf16[64,4096]{1,0:T(8,128)(2,1)S(1)}, u32[]{:S(2)}, u32[]{:S(2)}) %collective-permute-start.55) | collective-permute-done | bytes 524320 | tf_op jit(solution)/shard_map/ppermute | solution.py:359
  865.4 10.5 %collective-permute-done.63 = bf16[1,32,5248]{2,1,0:T(8,128)(2,1)S(1)} collective-permute-done((bf16[1,32,5248]{2,1,0:T(8,128)(2,1)S(1)}, bf16[1,32,5248]{2,1,0:T(8,128)(2,1)S(1)}, u32[]{:S(2)}, u32[]{:S(2)}) %collective-permute-start.63) | collective-permute-done | bytes 335904 | tf_op jit(solution)/shard_map/ppermute | solution.py:448
  877.1 16.6 %collective-permute-done.66 = bf16[2,32,5248]{2,1,0:T(8,128)(2,1)S(1)} collective-permute-done((bf16[2,32,5248]{2,1,0:T(8,128)(2,1)S(1)}, bf16[2,32,5248]{2,1,0:T(8,128)(2,1)S(1)}, u32[]{:S(2)}, u32[]{:S(2)}) %collective-permute-start.66) | collective-permute-done | bytes 671776 | tf_op jit(solution)/shard_map/ppermute | solution.py:448
  910.6 16.4 %collective-permute-done.59 = bf16[256,2048]{1,0:T(8,128)(2,1)} collective-permute-done((bf16[256,2048]{1,0:T(8,128)(2,1)}, bf16[256,2048]{1,0:T(8,128)(2,1)}, u32[]{:S(2)}, u32[]{:S(2)}) %collective-permute-start.59) | collective-permute-done | bytes 1048608 | tf_op jit(solution)/shard_map/ppermute | solution.py:426
  931.2 12.1 %convert_element_type.187 = f32[2048,2048]{1,0:T(8,128)} convert(bf16[2048,2048]{1,0:T(8,128)(2,1)} %all-gather.17.cloned.1.call-done) | non-fusion elementwise | flops 4194304 | bytes 25165824 | tf_op jit(solution)/shard_map/convert_element_type | solution.py:680
  966.4 17.7 %convert_element_type.190 = f32[512,2,8192]{2,1,0:T(2,128)} convert(bf16[512,2,8192]{2,1,0:T(2,128)(2,1)} %all-gather.19.cloned.1.call-done) | non-fusion elementwise | flops 8388608 | bytes 50331648 | tf_op jit(solution)/shard_map/convert_element_type | solution.py:679
  (581 shorter events, 511.4 us)
Async XLA Ops:
  7.2 163.7 %all-gather.11.cloned.1.call-start = ((), (), s32[]{:S(2)}) async-start(), calls=%async_computation.8 | async-start | bytes 3538944 | tf_op jit(solution)/shard_map/all_gather | solution.py:498
  7.2 59.2 %collective-permute-start.9 = (bf16[256,2048]{1,0:T(8,128)(2,1)}, bf16[256,2048]{1,0:T(8,128)(2,1)S(1)}, u32[]{:S(2)}, u32[]{:S(2)}) collective-permute-start(bf16[256,2048]{1,0:T(8,128)(2,1)} %param.11), channel_id=1, source_target_pairs={{0,1},{1,2},{2,3},{4,5},{5,6},{6,7},{8,9},{9,10},{10,11},{12,13},{... | collective-permute-start | bytes 3145736 | tf_op jit(solution)/shard_map/ppermute | solution.py:402
  12.4 54.0 %collective-permute-start.10 = (bf16[256,2048]{1,0:T(8,128)(2,1)}, bf16[256,2048]{1,0:T(8,128)(2,1)}, u32[]{:S(2)}, u32[]{:S(2)}) collective-permute-start(bf16[256,2048]{1,0:T(8,128)(2,1)} %param.11), channel_id=1, source_target_pairs={{1,0},{2,1},{3,2},{5,4},{6,5},{7,6},{9,8},{10,9},{11,10},{13,12},{... | collective-permute-start | bytes 3145736 | tf_op jit(solution)/shard_map/ppermute | solution.py:403
  69.6 162.2 %all-gather.13.cloned.1.call-start = ((), (), s32[]{:S(2)}) async-start(), calls=%async_computation.9 | async-start | bytes 9437184 | tf_op jit(solution)/shard_map/all_gather | solution.py:498
  71.7 239.3 %all-gather.15.cloned.1.call-start = ((), (), s32[]{:S(2)}) async-start(), calls=%async_computation.10 | async-start | bytes 18874368 | tf_op jit(solution)/shard_map/all_gather | solution.py:498
  154.5 48.3 %collective-permute-start.22 = (bf16[512,512]{1,0:T(8,128)(2,1)}, bf16[512,512]{1,0:T(8,128)(2,1)}, u32[]{:S(2)}, u32[]{:S(2)}) collective-permute-start(bf16[512,512]{1,0:T(8,128)(2,1)} %get-tuple-element.193), channel_id=1, source_target_pairs={{0,1},{1,0},{2,3},{3,2},{4,5},{5,4},{6,7},{7,6},{8,9},{9,8},{10,11... | collective-permute-start | bytes 1572872 | tf_op jit(solution)/shard_map/ppermute | solution.py:359
  157.1 45.7 %collective-permute-start.23 = (bf16[512,512]{1,0:T(8,128)(2,1)}, bf16[512,512]{1,0:T(8,128)(2,1)}, u32[]{:S(2)}, u32[]{:S(2)}) collective-permute-start(bf16[512,512]{1,0:T(8,128)(2,1)} %get-tuple-element.192), channel_id=1, source_target_pairs={{0,2},{1,3},{2,0},{3,1},{4,6},{5,7},{6,4},{7,5},{8,10},{9,11},{10,... | collective-permute-start | bytes 1572872 | tf_op jit(solution)/shard_map/ppermute | solution.py:359
  158.5 44.3 %collective-permute-start.24 = (bf16[512,512]{1,0:T(8,128)(2,1)}, bf16[512,512]{1,0:T(8,128)(2,1)}, u32[]{:S(2)}, u32[]{:S(2)}) collective-permute-start(bf16[512,512]{1,0:T(8,128)(2,1)} %get-tuple-element.191), channel_id=1, source_target_pairs={{0,3},{1,2},{2,1},{3,0},{4,7},{5,6},{6,5},{7,4},{8,11},{9,10},{10,... | collective-permute-start | bytes 1572872 | tf_op jit(solution)/shard_map/ppermute | solution.py:359
  206.0 419.3 %reduce-scatter.7.cloned.1.call-start = ((), (), s32[]{:S(2)}) async-start(), calls=%async_computation.5 | async-start | bytes 9437184 | tf_op jit(solution)/shard_map/reduce_scatter | solution.py:589
  254.4 45.0 %collective-permute-start.31 = (bf16[256,2048]{1,0:T(8,128)(2,1)S(1)}, bf16[256,2048]{1,0:T(8,128)(2,1)}, u32[]{:S(2)}, u32[]{:S(2)}) collective-permute-start(bf16[256,2048]{1,0:T(8,128)(2,1)S(1)} %copy-done.7), channel_id=1, source_target_pairs={{1,0},{2,1},{5,4},{6,5},{9,8},{10,9},{13,12},{14,13},{17,16},{18,1... | collective-permute-start | bytes 3145736 | tf_op jit(solution)/shard_map/ppermute | solution.py:403
  299.5 51.1 %collective-permute-start.32 = (bf16[256,2048]{1,0:T(8,128)(2,1)}, bf16[256,2048]{1,0:T(8,128)(2,1)}, u32[]{:S(2)}, u32[]{:S(2)}) collective-permute-start(bf16[256,2048]{1,0:T(8,128)(2,1)} %get-tuple-element.98), channel_id=1, source_target_pairs={{2,3},{6,7},{10,11},{14,15},{18,19},{22,23},{26,27},{30,31}} | collective-permute-start | bytes 3145736 | tf_op jit(solution)/shard_map/ppermute | solution.py:402
  301.1 49.4 %collective-permute-start.33 = (bf16[256,2048]{1,0:T(8,128)(2,1)}, bf16[256,2048]{1,0:T(8,128)(2,1)}, u32[]{:S(2)}, u32[]{:S(2)}) collective-permute-start(bf16[256,2048]{1,0:T(8,128)(2,1)} %get-tuple-element.99), channel_id=1, source_target_pairs={{1,0},{5,4},{9,8},{13,12},{17,16},{21,20},{25,24},{29,28}} | collective-permute-start | bytes 3145736 | tf_op jit(solution)/shard_map/ppermute | solution.py:403
  304.2 43.4 %collective-permute-start.27 = (bf16[256,2048]{1,0:T(8,128)(2,1)}, bf16[256,2048]{1,0:T(8,128)(2,1)}, u32[]{:S(2)}, u32[]{:S(2)}) collective-permute-start(bf16[256,2048]{1,0:T(8,128)(2,1)} %collective-permute-done.21.high_ref), channel_id=1, source_target_pairs={{1,0},{2,1},{5,4},{6,5},{9,8},{10,9},{13,12},{14,13},{17,16},{18,1... | collective-permute-start | bytes 3145736 | tf_op jit(solution)/shard_map/ppermute | solution.py:403
  425.0 200.3 %reduce-scatter.5.cloned.1.call-start = ((), (), s32[]{:S(2)}) async-start(), calls=%async_computation.4 | async-start | bytes 18874368 | tf_op jit(solution)/shard_map/reduce_scatter | solution.py:589
  430.5 72.2 %collective-permute-start.34 = (bf16[256,2048]{1,0:T(8,128)(2,1)}, bf16[256,2048]{1,0:T(8,128)(2,1)S(1)}, u32[]{:S(2)}, u32[]{:S(2)}) collective-permute-start(bf16[256,2048]{1,0:T(8,128)(2,1)} %get-tuple-element.184), channel_id=1, source_target_pairs={{0,2},{1,3},{2,0},{3,1},{4,6},{5,7},{6,4},{7,5},{8,10},{9,11},{10,... | collective-permute-start | bytes 3145736 | tf_op jit(solution)/shard_map/ppermute | solution.py:359
  430.5 72.2 %collective-permute-start.35 = (bf16[256,2048]{1,0:T(8,128)(2,1)}, bf16[256,2048]{1,0:T(8,128)(2,1)}, u32[]{:S(2)}, u32[]{:S(2)}) collective-permute-start(bf16[256,2048]{1,0:T(8,128)(2,1)} %get-tuple-element.183), channel_id=1, source_target_pairs={{0,3},{1,2},{2,1},{3,0},{4,7},{5,6},{6,5},{7,4},{8,11},{9,10},{10,... | collective-permute-start | bytes 3145736 | tf_op jit(solution)/shard_map/ppermute | solution.py:359
  467.6 263.7 %reduce-scatter.9.cloned.1.call-start = ((), (), s32[]{:S(2)}) async-start(), calls=%async_computation.6 | async-start | bytes 3538944 | tf_op jit(solution)/shard_map/reduce_scatter | solution.py:589
  538.9 52.4 %collective-permute-start.39 = (bf16[256,2048]{1,0:T(8,128)(2,1)}, bf16[256,2048]{1,0:T(8,128)(2,1)S(1)}, u32[]{:S(2)}, u32[]{:S(2)}) collective-permute-start(bf16[256,2048]{1,0:T(8,128)(2,1)} %after.41), channel_id=1, source_target_pairs={{0,1},{1,2},{2,3},{4,5},{5,6},{6,7},{8,9},{9,10},{10,11},{12,13},{... | collective-permute-start | bytes 3145736 | tf_op jit(solution)/shard_map/ppermute | solution.py:402
  542.9 49.1 %collective-permute-start.40 = (bf16[256,2048]{1,0:T(8,128)(2,1)}, bf16[256,2048]{1,0:T(8,128)(2,1)S(1)}, u32[]{:S(2)}, u32[]{:S(2)}) collective-permute-start(bf16[256,2048]{1,0:T(8,128)(2,1)} %after.41), channel_id=1, source_target_pairs={{1,0},{2,1},{3,2},{5,4},{6,5},{7,6},{9,8},{10,9},{11,10},{13,12},{... | collective-permute-start | bytes 3145736 | tf_op jit(solution)/shard_map/ppermute | solution.py:403
  625.4 107.1 %all-gather.17.cloned.1.call-start = ((), (), s32[]{:S(2)}) async-start(), calls=%async_computation.11 | async-start | bytes 9437184 | tf_op jit(solution)/shard_map/all_gather | solution.py:498
  626.1 207.3 %reduce-scatter.11.cloned.1.call-start = ((), (), s32[]{:S(2)}) async-start(), calls=%async_computation.7 | async-start | bytes 2949120 | tf_op jit(solution)/shard_map/reduce_scatter | solution.py:589
  743.6 222.8 %all-gather.19.cloned.1.call-start = ((), (), s32[]{:S(2)}) async-start(), calls=%async_computation.12 | async-start | bytes 18874368 | tf_op jit(solution)/shard_map/all_gather | solution.py:498
  769.3 47.6 %collective-permute-start.55 = (bf16[64,4096]{1,0:T(8,128)(2,1)S(1)}, bf16[64,4096]{1,0:T(8,128)(2,1)S(1)}, u32[]{:S(2)}, u32[]{:S(2)}) collective-permute-start(bf16[64,4096]{1,0:T(8,128)(2,1)S(1)} %get-tuple-element.180), channel_id=1, source_target_pairs={{0,3},{1,2},{2,1},{3,0},{4,7},{5,6},{6,5},{7,4},{8,11},{9,10},{10,... | collective-permute-start | bytes 1572872 | tf_op jit(solution)/shard_map/ppermute | solution.py:359
  897.5 47.2 %collective-permute-start.67 = (bf16[4,64,5248]{2,1,0:T(8,128)(2,1)}, bf16[4,64,5248]{2,1,0:T(8,128)(2,1)}, u32[]{:S(2)}, u32[]{:S(2)}) collective-permute-start(bf16[4,64,5248]{2,1,0:T(8,128)(2,1)} %maximum_maximum_fusion), channel_id=1, source_target_pairs={{0,4},{4,0},{8,12},{12,8},{16,20},{20,16},{24,28},{28,24},{1,5},{5... | collective-permute-start | bytes 8060936 | tf_op jit(solution)/shard_map/ppermute | solution.py:448
  (159 other events, 2347.6 us)
Sparse Core Ops, SparseCore 0:
  69.7 35.0 all-gather.10
  107.2 54.3 all-gather.12
  206.2 91.7 all-gather.14
  425.1 69.2 reduce-scatter.6
  498.9 115.9 reduce-scatter.4
  625.5 46.0 reduce-scatter.8
  673.5 54.3 all-gather.16
  743.7 42.2 reduce-scatter.10
  834.9 100.4 all-gather.18

commit v4 on v3

--- a/solution.py
+++ b/solution.py
@@ -638,7 +638,6 @@
     gu_grad, down_grad, qkv_grad = after((gu_grad, down_grad, qkv_grad), n1_hops[0])
     qkv_grad = sum_plane(qkv_grad)
     down_grad = over_plane(down_grad).reshape(ffs, width)
-    gu_grad = by_group(after(gu_grad, n1_hops[-2]))
     grad_n1 = sum(part.astype(F32) for part in (n1_slots[0], *n1_hops[-1]))
     grad_attn_all = line.gather(grad_attn, (), 0, ga_hops)
     inv1 = inverse_rms(x_own)
@@ -654,16 +653,17 @@
     out_grad = out_grad.reshape(replicas, rows, width)
     gain_grads = gain_grads.reshape(replicas, rows, groups * 128)
     out_grad = jnp.concatenate([out_grad, gain_grads], axis=2)
+    gu_grad = by_group(after(gu_grad, n1_hops[-2], out_grad))
     out_grad = sum_plane(after(out_grad, down_grad, qkv_grad))
     y_hops = []
     for hop in range(groups - 1, 0, -1):
-        gate = (n1_hops[-1], gu_grad[1:], ())[min(len(y_hops), 2)]
+        gate = () if y_hops else gu_grad[1:]
         y_hops.append(line.scatter_hop(down, y_hops[-1] if y_hops else None, hop, gate))
     mixed = (h1 + sum(part.astype(F32) for part in (down[0], *y_hops[-1]))).astype(BF16)
 
     gu_grad = line.ordered(gu_grad)
     gu_grad = jnp.concatenate([part.reshape(rows, 2, ffs) for part in gu_grad], axis=2)
-    gu_grad = over_plane(after(gu_grad, out_grad, y_hops[0]))
+    gu_grad = over_plane(after(gu_grad, out_grad))
 
     grads = jnp.concatenate(
         [qkv_grad.reshape(rows, groups, qkvw), out_grad[:, width:].reshape(rows, groups, 128)], axis=2

time: 1000 us -> 1020 us (1.020)
  waiting for transfers between devices: 333 us -> 353 us
    ppermute x12, starting transfers between devices: 27.6 us -> 15.9 us  [gather(): high.append(lax.ppermute(moving[1], 'group', down))]
    slice x37 -> x34, local copies, waits for them, and re-layouts: 35.6 us -> 31.2 us  [mark(): return value[:8, :128]]
  transfers between devices with their start and end apart: 77 -> 77, of which waited for: 33 -> 32; matrix products, arithmetic and copies ran while one was open for 26% -> 26% of each run, Pallas kernels for 12% -> 12%
where the time goes in v4:
time: 1020 us; the launch traced here: 1010 us
  waiting for transfers between devices  353 us (35%)
  Pallas kernels  170 us (17%)
  starting transfers between devices  147 us (14%)
  local copies, waits for them, and re-layouts  142 us (14%)
  other arithmetic  120 us (12%)
  matrix products  56.9 us (6%)
  between operations  16 us (2%)
    ppermute x27, waiting for transfers between devices, swap(): lax.ppermute(value, 'group', [(i, i ^ slot) for i in range(self.count)])  124 us
    ppermute x12, waiting for transfers between devices, gather(): high.append(lax.ppermute(moving[1], 'group', down))  117 us
    ppermute x27, starting transfers between devices, swap(): lax.ppermute(value, 'group', [(i, i ^ slot) for i in range(self.count)])  62.4 us
    pallas_call x2, Pallas kernels, feed_forward(): pl.pallas_call(functools.partial(hidden_kernel, parts), grid=(count // pa...  61.1 us
    pallas_call x2, Pallas kernels, weight_gradient(): pl.pallas_call(functools.partial(product_kernel, parts), grid=(blocks, le...  51 us
    dot_general x7, matrix products, dot(): lax.dot_general(left, right, (dims, ((), ())), preferred_element_type=F32)  46.5 us
    ppermute x5, waiting for transfers between devices, swap(): lax.ppermute(part, 'replica', [(i, i ^ bit) for i in range(replicas)])  39.8 us
    unnamed x243, local copies, waits for them, and re-layouts  38.2 us
  transfers between devices with their start and end apart: 77, of which 32 were waited for; matrix products, arithmetic and copies ran while one was open for 26% of the time, Pallas kernels for 12%

profile of v4, /device:TPU:0, one launch (start us, length us, event | category | flops | bytes accessed | tf_op | source)
XLA Modules:
  0.0 1005.6 jit_solution(10048652685135112507)
XLA Ops:
  24.1 18.4 %collective-permute-done.3.refs_1_ = bf16[64,768]{1,0:T(8,128)(2,1)S(1)} collective-permute-done((bf16[64,768]{1,0:T(8,128)(2,1)S(1)}, bf16[64,768]{1,0:T(8,128)(2,1)S(1)}, u32[]{:S(2)}, u32[]{:S(2)}) %collective-permute-start.3) | collective-permute-done | bytes 98336 | tf_op jit(solution)/shard_map/ppermute | solution.py:359
  97.2 13.2 %collective-permute-done.12 = bf16[256,2048]{1,0:T(8,128)(2,1)} collective-permute-done((bf16[256,2048]{1,0:T(8,128)(2,1)}, bf16[256,2048]{1,0:T(8,128)(2,1)}, u32[]{:S(2)}, u32[]{:S(2)}) %collective-permute-start.12) | collective-permute-done | bytes 1048608 | tf_op jit(solution)/shard_map/ppermute | solution.py:403
  116.9 18.1 %collective-permute-done.14 = bf16[256,2048]{1,0:T(8,128)(2,1)S(1)} collective-permute-done((bf16[256,2048]{1,0:T(8,128)(2,1)}, bf16[256,2048]{1,0:T(8,128)(2,1)S(1)}, u32[]{:S(2)}, u32[]{:S(2)}) %collective-permute-start.14) | collective-permute-done | bytes 1048608 | tf_op jit(solution)/shard_map/ppermute | solution.py:403
  175.8 21.8 %attention_forward.1 = (bf16[1024,512]{1,0:T(8,128)(2,1)}, bf16[1024,128]{1,0:T(8,128)(2,1)}, bf16[1024,128]{1,0:T(8,128)(2,1)}, f32[1024,512]{1,0:T(8,128)}, f3...) custom-call(f32[1024,768]{1,0:T(8,128)} %fusion.91.qkv_ref, f32[1024,128]{1,0:T(8,128)} %copy.171.cos_ref, ...), custom_call_target="tpu_custom_call" | custom-call | flops 1 | bytes 1 | tf_op jit(solution)/shard_map/attention_forward/pallas_call | solution.py:169
  256.3 15.9 %collective-permute-done.20.low_ref = bf16[256,2048]{1,0:T(8,128)(2,1)} collective-permute-done((bf16[256,2048]{1,0:T(8,128)(2,1)S(1)}, bf16[256,2048]{1,0:T(8,128)(2,1)}, u32[]{:S(2)}, u32[]{:S(2)}) %collective-permute-start.20) | collective-permute-done | bytes 1048608 | tf_op jit(solution)/shard_map/ppermute | solution.py:402
  282.7 17.3 %collective-permute-done.31.refs_1_ = bf16[256,2048]{1,0:T(8,128)(2,1)} collective-permute-done((bf16[256,2048]{1,0:T(8,128)(2,1)S(1)}, bf16[256,2048]{1,0:T(8,128)(2,1)}, u32[]{:S(2)}, u32[]{:S(2)}) %collective-permute-start.31) | collective-permute-done | bytes 1048608 | tf_op jit(solution)/shard_map/ppermute | solution.py:403
  311.6 30.5 %feed_forward.2 = (bf16[512,2048]{1,0:T(8,128)(2,1)}, bf16[512,2048]{1,0:T(8,128)(2,1)}, bf16[512,2048]{1,0:T(8,128)(2,1)}, bf16[512,2048]{1,0:T(8,128)(2,1)}) custom-call(bf16[512,2048]{1,0:T(8,128)(2,1)} %copy-done.2, bf16[512,2048]{1,0:T(8,128)(2,1)} %copy-done.10, bf16[8,2048,512]{2,1,0:T(8,128)(2,1)} %bitcast.180, bf16[2048,2048]{1,0:T(8,128)(2,1)} %down_ref.3), custom_call_target="tpu_custom_call" | custom-call | flops 299999985664 | bytes 1 | tf_op jit(solution)/shard_map/feed_forward/pallas_call | solution.py:245
  355.2 18.6 %collective-permute-done.29 = bf16[256,2048]{1,0:T(8,128)(2,1)} collective-permute-done((bf16[256,2048]{1,0:T(8,128)(2,1)}, bf16[256,2048]{1,0:T(8,128)(2,1)}, u32[]{:S(2)}, u32[]{:S(2)}) %collective-permute-start.29) | collective-permute-done | bytes 1048608 | tf_op jit(solution)/shard_map/ppermute | solution.py:403
  378.3 30.6 %feed_forward.3 = (bf16[512,2048]{1,0:T(8,128)(2,1)}, bf16[512,2048]{1,0:T(8,128)(2,1)}, bf16[512,2048]{1,0:T(8,128)(2,1)}, bf16[512,2048]{1,0:T(8,128)(2,1)}) custom-call(bf16[512,2048]{1,0:T(8,128)(2,1)} %after.32.n2_ref.refs_1_, bf16[512,2048]{1,0:T(8,128)(2,1)} %pad_maximum_fusion.5.dy_ref.refs_3_, bf16[8,2048,512]{2,1,0:T(8,128)(2,1)} %bitcast.181, ...), custom_call_target="tpu_custom_call" | custom-call | flops 1 | bytes 1 | tf_op jit(solution)/shard_map/feed_forward/pallas_call | solution.py:245
  409.0 17.6 %weight_gradient.2 = (bf16[2048,2048]{1,0:T(8,128)(2,1)}, f32[8,128]{1,0:T(8,128)}) custom-call(bf16[512,2048]{1,0:T(8,128)(2,1)} %get-tuple-element.85.refs_0_, bf16[512,2048]{1,0:T(8,128)(2,1)} %get-tuple-element.101.refs_1_.refs_0_, bf16[512,2048]{1,0:T(8,128)(2,1)} %copy-done.10, bf16[512,2048]{1,0:T(8,128)(2,1)} %pad_maximum_fusion.5.dy_ref.refs_3_), custom_call_target="tpu_custom_call" | custom-call | flops 1 | bytes 1 | tf_op jit(solution)/shard_map/weight_gradient/pallas_call | solution.py:304
  435.6 33.4 %weight_gradient.3 = (bf16[8,4,64,4096]{3,2,1,0:T(8,128)(2,1)}, f32[8,128]{1,0:T(8,128)}) custom-call(bf16[512,2048]{1,0:T(8,128)(2,1)} %after.36.refs_0_, bf16[512,2048]{1,0:T(8,128)(2,1)} %after.32.n2_ref.refs_1_, bf16[512,2048]{1,0:T(8,128)(2,1)} %get-tuple-element.103.refs_2_, bf16[512,2048]{1,0:T(8,128)(2,1)} %get-tuple-element.104.refs_3_, ...), custom_call_target="tpu_custom_call" | custom-call | flops 1 | bytes 1 | tf_op jit(solution)/shard_map/weight_gradient/pallas_call | solution.py:304
  469.5 34.7 %collective-permute-done.34.refs_2_ = bf16[256,2048]{1,0:T(8,128)(2,1)S(1)} collective-permute-done((bf16[256,2048]{1,0:T(8,128)(2,1)}, bf16[256,2048]{1,0:T(8,128)(2,1)S(1)}, u32[]{:S(2)}, u32[]{:S(2)}) %collective-permute-start.34) | collective-permute-done | bytes 1048608 | tf_op jit(solution)/shard_map/ppermute | solution.py:359
  521.7 17.6 %collective-permute-start.37 = (bf16[256,512]{1,0:T(8,128)(2,1)}, bf16[256,512]{1,0:T(8,128)(2,1)}, u32[]{:S(2)}, u32[]{:S(2)}) collective-permute-start(bf16[256,512]{1,0:T(8,128)(2,1)} %get-tuple-element.194), channel_id=1, source_target_pairs={{0,2},{1,3},{2,0},{3,1},{4,6},{5,7},{6,4},{7,5},{8,10},{9,11},{10,... | collective-permute-start | bytes 786440 | tf_op jit(solution)/shard_map/ppermute | solution.py:359
  557.4 34.7 %attention_backward.1 = (bf16[1024,768]{1,0:T(8,128)(2,1)}, bf16[1024,768]{1,0:T(8,128)(2,1)}) custom-call(bf16[1024,512]{1,0:T(8,128)(2,1)} %get-tuple-element.86.q_ref, bf16[1024,128]{1,0:T(8,128)(2,1)} %get-tuple-element.87.k_ref, bf16[1024,128]{1,0:T(8,128)(2,1)} %get-tuple-element.88.v_ref, f32[1024,512]{1,0:T(8,128)} %get-tuple-element.89.att_ref, ...), custom_call_target="tpu_custom_call" | custom-call | flops 40000000000 | bytes 1 | tf_op jit(solution)/shard_map/attention_backward/pallas_call | solution.py:187
  633.1 24.4 %collective-permute-done.44.refs_1_ = bf16[256,2048]{1,0:T(8,128)(2,1)S(1)} collective-permute-done((bf16[256,2048]{1,0:T(8,128)(2,1)}, bf16[256,2048]{1,0:T(8,128)(2,1)S(1)}, u32[]{:S(2)}, u32[]{:S(2)}) %collective-permute-start.44) | collective-permute-done | bytes 1048608 | tf_op jit(solution)/shard_map/ppermute | solution.py:403
  706.8 10.6 %collective-permute-done.50 = bf16[256,2048]{1,0:T(8,128)(2,1)S(1)} collective-permute-done((bf16[256,2048]{1,0:T(8,128)(2,1)}, bf16[256,2048]{1,0:T(8,128)(2,1)S(1)}, u32[]{:S(2)}, u32[]{:S(2)}) %collective-permute-start.50) | collective-permute-done | bytes 1048608 | tf_op jit(solution)/shard_map/ppermute | solution.py:426
  749.8 14.4 %collective-permute-done.51 = bf16[64,4096]{1,0:T(8,128)(2,1)S(1)} collective-permute-done((bf16[64,4096]{1,0:T(8,128)(2,1)S(1)}, bf16[64,4096]{1,0:T(8,128)(2,1)S(1)}, u32[]{:S(2)}, u32[]{:S(2)}) %collective-permute-start.51) | collective-permute-done | bytes 524320 | tf_op jit(solution)/shard_map/ppermute | solution.py:359
  764.2 19.3 %collective-permute-done.52 = bf16[64,4096]{1,0:T(8,128)(2,1)S(1)} collective-permute-done((bf16[64,4096]{1,0:T(8,128)(2,1)S(1)}, bf16[64,4096]{1,0:T(8,128)(2,1)S(1)}, u32[]{:S(2)}, u32[]{:S(2)}) %collective-permute-start.52) | collective-permute-done | bytes 524320 | tf_op jit(solution)/shard_map/ppermute | solution.py:359
  848.7 13.3 %collective-permute-done.54 = bf16[256,2048]{1,0:T(8,128)(2,1)S(1)} collective-permute-done((bf16[256,2048]{1,0:T(8,128)(2,1)}, bf16[256,2048]{1,0:T(8,128)(2,1)S(1)}, u32[]{:S(2)}, u32[]{:S(2)}) %collective-permute-start.54) | collective-permute-done | bytes 1048608 | tf_op jit(solution)/shard_map/ppermute | solution.py:426
  869.6 15.7 %collective-permute-done.63 = bf16[1,32,5248]{2,1,0:T(8,128)(2,1)S(1)} collective-permute-done((bf16[1,32,5248]{2,1,0:T(8,128)(2,1)S(1)}, bf16[1,32,5248]{2,1,0:T(8,128)(2,1)S(1)}, u32[]{:S(2)}, u32[]{:S(2)}) %collective-permute-start.63) | collective-permute-done | bytes 335904 | tf_op jit(solution)/shard_map/ppermute | solution.py:448
  887.4 23.4 %collective-permute-done.66 = bf16[2,32,5248]{2,1,0:T(8,128)(2,1)S(1)} collective-permute-done((bf16[2,32,5248]{2,1,0:T(8,128)(2,1)S(1)}, bf16[2,32,5248]{2,1,0:T(8,128)(2,1)S(1)}, u32[]{:S(2)}, u32[]{:S(2)}) %collective-permute-start.66) | collective-permute-done | bytes 671776 | tf_op jit(solution)/shard_map/ppermute | solution.py:448
  926.1 16.7 %collective-permute-done.59 = bf16[256,2048]{1,0:T(8,128)(2,1)} collective-permute-done((bf16[256,2048]{1,0:T(8,128)(2,1)}, bf16[256,2048]{1,0:T(8,128)(2,1)}, u32[]{:S(2)}, u32[]{:S(2)}) %collective-permute-start.59) | collective-permute-done | bytes 1048608 | tf_op jit(solution)/shard_map/ppermute | solution.py:426
  947.1 11.8 %convert_element_type.187 = f32[2048,2048]{1,0:T(8,128)} convert(bf16[2048,2048]{1,0:T(8,128)(2,1)} %all-gather.17.cloned.1.call-done) | non-fusion elementwise | flops 4194304 | bytes 25165824 | tf_op jit(solution)/shard_map/convert_element_type | solution.py:680
  981.1 17.7 %convert_element_type.190 = f32[512,2,8192]{2,1,0:T(2,128)} convert(bf16[512,2,8192]{2,1,0:T(2,128)(2,1)} %all-gather.19.cloned.1.call-done) | non-fusion elementwise | flops 8388608 | bytes 50331648 | tf_op jit(solution)/shard_map/convert_element_type | solution.py:679
  (578 shorter events, 499.7 us)
Async XLA Ops:
  7.2 155.5 %all-gather.11.cloned.1.call-start = ((), (), s32[]{:S(2)}) async-start(), calls=%async_computation.8 | async-start | bytes 3538944 | tf_op jit(solution)/shard_map/all_gather | solution.py:498
  7.2 59.2 %collective-permute-start.9 = (bf16[256,2048]{1,0:T(8,128)(2,1)}, bf16[256,2048]{1,0:T(8,128)(2,1)S(1)}, u32[]{:S(2)}, u32[]{:S(2)}) collective-permute-start(bf16[256,2048]{1,0:T(8,128)(2,1)} %param.11), channel_id=1, source_target_pairs={{0,1},{1,2},{2,3},{4,5},{5,6},{6,7},{8,9},{9,10},{10,11},{12,13},{... | collective-permute-start | bytes 3145736 | tf_op jit(solution)/shard_map/ppermute | solution.py:402
  12.4 54.0 %collective-permute-start.10 = (bf16[256,2048]{1,0:T(8,128)(2,1)}, bf16[256,2048]{1,0:T(8,128)(2,1)}, u32[]{:S(2)}, u32[]{:S(2)}) collective-permute-start(bf16[256,2048]{1,0:T(8,128)(2,1)} %param.11), channel_id=1, source_target_pairs={{1,0},{2,1},{3,2},{5,4},{6,5},{7,6},{9,8},{10,9},{11,10},{13,12},{... | collective-permute-start | bytes 3145736 | tf_op jit(solution)/shard_map/ppermute | solution.py:403
  69.6 161.6 %all-gather.13.cloned.1.call-start = ((), (), s32[]{:S(2)}) async-start(), calls=%async_computation.9 | async-start | bytes 9437184 | tf_op jit(solution)/shard_map/all_gather | solution.py:498
  71.7 239.8 %all-gather.15.cloned.1.call-start = ((), (), s32[]{:S(2)}) async-start(), calls=%async_computation.10 | async-start | bytes 18874368 | tf_op jit(solution)/shard_map/all_gather | solution.py:498
  142.8 56.0 %collective-permute-start.22 = (bf16[512,512]{1,0:T(8,128)(2,1)}, bf16[512,512]{1,0:T(8,128)(2,1)}, u32[]{:S(2)}, u32[]{:S(2)}) collective-permute-start(bf16[512,512]{1,0:T(8,128)(2,1)} %get-tuple-element.189), channel_id=1, source_target_pairs={{0,1},{1,0},{2,3},{3,2},{4,5},{5,4},{6,7},{7,6},{8,9},{9,8},{10,11... | collective-permute-start | bytes 1572872 | tf_op jit(solution)/shard_map/ppermute | solution.py:359
  145.4 54.2 %collective-permute-start.23 = (bf16[512,512]{1,0:T(8,128)(2,1)}, bf16[512,512]{1,0:T(8,128)(2,1)}, u32[]{:S(2)}, u32[]{:S(2)}) collective-permute-start(bf16[512,512]{1,0:T(8,128)(2,1)} %get-tuple-element.188), channel_id=1, source_target_pairs={{0,2},{1,3},{2,0},{3,1},{4,6},{5,7},{6,4},{7,5},{8,10},{9,11},{10,... | collective-permute-start | bytes 1572872 | tf_op jit(solution)/shard_map/ppermute | solution.py:359
  146.8 52.9 %collective-permute-start.24 = (bf16[512,512]{1,0:T(8,128)(2,1)}, bf16[512,512]{1,0:T(8,128)(2,1)}, u32[]{:S(2)}, u32[]{:S(2)}) collective-permute-start(bf16[512,512]{1,0:T(8,128)(2,1)} %get-tuple-element.187), channel_id=1, source_target_pairs={{0,3},{1,2},{2,1},{3,0},{4,7},{5,6},{6,5},{7,4},{8,11},{9,10},{10,... | collective-permute-start | bytes 1572872 | tf_op jit(solution)/shard_map/ppermute | solution.py:359
  202.9 425.5 %reduce-scatter.7.cloned.1.call-start = ((), (), s32[]{:S(2)}) async-start(), calls=%async_computation.5 | async-start | bytes 9437184 | tf_op jit(solution)/shard_map/reduce_scatter | solution.py:589
  254.4 45.5 %collective-permute-start.31 = (bf16[256,2048]{1,0:T(8,128)(2,1)S(1)}, bf16[256,2048]{1,0:T(8,128)(2,1)}, u32[]{:S(2)}, u32[]{:S(2)}) collective-permute-start(bf16[256,2048]{1,0:T(8,128)(2,1)S(1)} %copy-done.7), channel_id=1, source_target_pairs={{1,0},{2,1},{5,4},{6,5},{9,8},{10,9},{13,12},{14,13},{17,16},{18,1... | collective-permute-start | bytes 3145736 | tf_op jit(solution)/shard_map/ppermute | solution.py:403
  300.0 51.6 %collective-permute-start.32 = (bf16[256,2048]{1,0:T(8,128)(2,1)}, bf16[256,2048]{1,0:T(8,128)(2,1)}, u32[]{:S(2)}, u32[]{:S(2)}) collective-permute-start(bf16[256,2048]{1,0:T(8,128)(2,1)} %get-tuple-element.96), channel_id=1, source_target_pairs={{2,3},{6,7},{10,11},{14,15},{18,19},{22,23},{26,27},{30,31}} | collective-permute-start | bytes 3145736 | tf_op jit(solution)/shard_map/ppermute | solution.py:402
  301.6 50.0 %collective-permute-start.33 = (bf16[256,2048]{1,0:T(8,128)(2,1)}, bf16[256,2048]{1,0:T(8,128)(2,1)}, u32[]{:S(2)}, u32[]{:S(2)}) collective-permute-start(bf16[256,2048]{1,0:T(8,128)(2,1)} %get-tuple-element.97), channel_id=1, source_target_pairs={{1,0},{5,4},{9,8},{13,12},{17,16},{21,20},{25,24},{29,28}} | collective-permute-start | bytes 3145736 | tf_op jit(solution)/shard_map/ppermute | solution.py:403
  426.6 201.8 %reduce-scatter.5.cloned.1.call-start = ((), (), s32[]{:S(2)}) async-start(), calls=%async_computation.4 | async-start | bytes 18874368 | tf_op jit(solution)/shard_map/reduce_scatter | solution.py:589
  432.0 72.1 %collective-permute-start.34 = (bf16[256,2048]{1,0:T(8,128)(2,1)}, bf16[256,2048]{1,0:T(8,128)(2,1)S(1)}, u32[]{:S(2)}, u32[]{:S(2)}) collective-permute-start(bf16[256,2048]{1,0:T(8,128)(2,1)} %get-tuple-element.180), channel_id=1, source_target_pairs={{0,2},{1,3},{2,0},{3,1},{4,6},{5,7},{6,4},{7,5},{8,10},{9,11},{10,... | collective-permute-start | bytes 3145736 | tf_op jit(solution)/shard_map/ppermute | solution.py:359
  432.0 72.2 %collective-permute-start.35 = (bf16[256,2048]{1,0:T(8,128)(2,1)}, bf16[256,2048]{1,0:T(8,128)(2,1)}, u32[]{:S(2)}, u32[]{:S(2)}) collective-permute-start(bf16[256,2048]{1,0:T(8,128)(2,1)} %get-tuple-element.179), channel_id=1, source_target_pairs={{0,3},{1,2},{2,1},{3,0},{4,7},{5,6},{6,5},{7,4},{8,11},{9,10},{10,... | collective-permute-start | bytes 3145736 | tf_op jit(solution)/shard_map/ppermute | solution.py:359
  469.0 267.3 %reduce-scatter.9.cloned.1.call-start = ((), (), s32[]{:S(2)}) async-start(), calls=%async_computation.6 | async-start | bytes 3538944 | tf_op jit(solution)/shard_map/reduce_scatter | solution.py:589
  540.9 52.6 %collective-permute-start.39 = (bf16[256,2048]{1,0:T(8,128)(2,1)}, bf16[256,2048]{1,0:T(8,128)(2,1)S(1)}, u32[]{:S(2)}, u32[]{:S(2)}) collective-permute-start(bf16[256,2048]{1,0:T(8,128)(2,1)} %after.40), channel_id=1, source_target_pairs={{0,1},{1,2},{2,3},{4,5},{5,6},{6,7},{8,9},{9,10},{10,11},{12,13},{... | collective-permute-start | bytes 3145736 | tf_op jit(solution)/shard_map/ppermute | solution.py:402
  544.8 49.2 %collective-permute-start.40 = (bf16[256,2048]{1,0:T(8,128)(2,1)}, bf16[256,2048]{1,0:T(8,128)(2,1)S(1)}, u32[]{:S(2)}, u32[]{:S(2)}) collective-permute-start(bf16[256,2048]{1,0:T(8,128)(2,1)} %after.40), channel_id=1, source_target_pairs={{1,0},{2,1},{3,2},{5,4},{6,5},{7,6},{9,8},{10,9},{11,10},{13,12},{... | collective-permute-start | bytes 3145736 | tf_op jit(solution)/shard_map/ppermute | solution.py:403
  628.4 109.2 %all-gather.17.cloned.1.call-start = ((), (), s32[]{:S(2)}) async-start(), calls=%async_computation.11 | async-start | bytes 9437184 | tf_op jit(solution)/shard_map/all_gather | solution.py:498
  629.1 171.1 %reduce-scatter.11.cloned.1.call-start = ((), (), s32[]{:S(2)}) async-start(), calls=%async_computation.7 | async-start | bytes 2949120 | tf_op jit(solution)/shard_map/reduce_scatter | solution.py:589
  738.9 242.2 %all-gather.19.cloned.1.call-start = ((), (), s32[]{:S(2)}) async-start(), calls=%async_computation.12 | async-start | bytes 18874368 | tf_op jit(solution)/shard_map/all_gather | solution.py:498
  862.3 51.1 %collective-permute-start.55 = (bf16[256,2048]{1,0:T(8,128)(2,1)S(1)}, bf16[256,2048]{1,0:T(8,128)(2,1)S(1)}, u32[]{:S(2)}, u32[]{:S(2)}) collective-permute-start(bf16[256,2048]{1,0:T(8,128)(2,1)S(1)} %get-tuple-element.160), channel_id=1, source_target_pairs={{0,1},{1,2},{4,5},{5,6},{8,9},{9,10},{12,13},{13,14},{16,17},{17,1... | collective-permute-start | bytes 3145736 | tf_op jit(solution)/shard_map/ppermute | solution.py:426
  866.7 46.8 %collective-permute-start.58 = (bf16[256,2048]{1,0:T(8,128)(2,1)S(1)}, bf16[256,2048]{1,0:T(8,128)(2,1)S(1)}, u32[]{:S(2)}, u32[]{:S(2)}) collective-permute-start(bf16[256,2048]{1,0:T(8,128)(2,1)S(1)} %get-tuple-element.161), channel_id=1, source_target_pairs={{2,1},{3,2},{6,5},{7,6},{10,9},{11,10},{14,13},{15,14},{18,17},{19... | collective-permute-start | bytes 3145736 | tf_op jit(solution)/shard_map/ppermute | solution.py:426
  913.3 46.0 %collective-permute-start.67 = (bf16[4,64,5248]{2,1,0:T(8,128)(2,1)}, bf16[4,64,5248]{2,1,0:T(8,128)(2,1)}, u32[]{:S(2)}, u32[]{:S(2)}) collective-permute-start(bf16[4,64,5248]{2,1,0:T(8,128)(2,1)} %maximum_maximum_fusion), channel_id=1, source_target_pairs={{0,4},{4,0},{8,12},{12,8},{16,20},{20,16},{24,28},{28,24},{1,5},{5... | collective-permute-start | bytes 8060936 | tf_op jit(solution)/shard_map/ppermute | solution.py:448
  (159 other events, 2475.1 us)
Sparse Core Ops, SparseCore 0:
  69.7 35.0 all-gather.10
  107.2 54.3 all-gather.12
  203.0 94.8 all-gather.14
  426.7 69.5 reduce-scatter.6
  500.6 115.9 reduce-scatter.4
  628.5 47.3 reduce-scatter.8
  677.8 54.3 all-gather.16
  739.0 45.0 reduce-scatter.10
  801.6 117.2 all-gather.18
